TPU v7x, 256 devices: a whole 4x4x8 slice. The times are simulated.
256 devices in a mesh: dp: 8 (over x, core), row: 4 (over y), col: 8 (over z).
Axes of the slice: x: 4, y: 4, z: 8, core: 2. Of those that a mesh axis runs over, the one named last changes fastest.
Arguments:
- grad: bfloat16 [8, 2, 8192, 1024], P('dp', None, 'row', 'col'), may hold values from -120 to 120
- momentum: float32 [8, 2, 8192, 1024], P('dp', None, 'row', 'col'), may hold values from -120 to 120
- right_factor: float32 [1024, 2, 256], P('col'), may hold values from -0.1875 to 0.1875
Outputs:
- momentum_next: float32 [8, 2, 8192, 1024], P('dp', None, 'row', 'col')
- update: bfloat16 [2, 8192, 1024], P(None, 'row', 'col')
- factor_next: float32 [1024, 2, 256], P('col')
All inputs are finite; a program needn't handle non-finite values.
Results may differ from a plain program's by a relative error of at most 0.001.
Values sent between devices are 32-bit elements; how exact they have to be, the bound alone decides.
No kernel may reach another device: no remote copies, remote signals or barrier semaphores. Data moves between devices by JAX's collectives and lax.ppermute only.
A program may use at most 64 MiB of HBM per device.

v0:
```python
import math

import jax
import jax.numpy as jnp
from jax import lax
from jax.experimental import pallas as pl
from jax.experimental.pallas import tpu as pltpu
from jax.sharding import Mesh, PartitionSpec as P

D = 8192
KV = 1024
RANK = 256
ITERS = 2
NX, NC, NY, NZ = 4, 2, 4, 8
BLOCK = 64
QUAD = 4
WIDTH = KV // NZ

epsilon = 1e-06
decay_keep = 0.1
highest = lax.Precision.HIGHEST


def dot(a, b, contract):
    return lax.dot_general(
        a, b, (contract, ((), ())), precision=highest, preferred_element_type=jnp.float32
    )


def small_inverse_factor(block):
    size = block.shape[0]
    count = size // 8
    chunks = [block[8 * c : 8 * c + 8] for c in range(count)]
    sub = lax.broadcasted_iota(jnp.int32, (8, size), 0)
    lane = lax.broadcasted_iota(jnp.int32, (8, size), 1)
    pivots = []
    for p in range(count):
        lo = 8 * p
        spread = {}
        for c in range(p, count):
            for k in range(8):
                spread[k, c] = jnp.broadcast_to(chunks[c][:, lo + k : lo + k + 1], (8, size))
        panel = (lane >= lo) & (lane < lo + 8)
        for c in range(p, count):
            unit = jnp.where(lane == sub + lo, 1.0, 0.0) if c == p else 0.0
            chunks[c] = jnp.where(panel, unit, chunks[c])
        held = None
        for j in range(8):
            pivot = jnp.broadcast_to(spread[j, p][j : j + 1, :], (8, size))
            held = pivot if held is None else jnp.where(sub >= j, pivot, held)
            scale = pltpu.reciprocal(pivot, approx=True)
            row = jnp.broadcast_to(chunks[p][j : j + 1, :], (8, size)) * scale
            heads = {
                k: jnp.broadcast_to(spread[k, p][j : j + 1, :], (8, size)) * scale
                for k in range(j + 1, 8)
            }
            for c in range(p, count):
                column = spread[j, c]
                if c == p:
                    column = jnp.where(sub > j, column, 0.0)
                chunks[c] = chunks[c] - column * row
                for k in heads:
                    spread[k, c] = spread[k, c] - column * heads[k]
        pivots.append(held)
    inverse = jnp.concatenate([c * lax.rsqrt(d) for c, d in zip(chunks, pivots)], axis=0)
    row_ids = lax.broadcasted_iota(jnp.int32, (size, size), 0)
    col_ids = lax.broadcasted_iota(jnp.int32, (size, size), 1)
    return jnp.where(col_ids <= row_ids, inverse, 0.0)


def inverse_factor(gram, out_ref):
    out_ref[...] = gram
    for lo in range(0, RANK, BLOCK):
        hi = lo + BLOCK
        rows = out_ref[lo:hi, :]
        inverse = small_inverse_factor(rows[:, lo:hi])
        scaled = dot(inverse, rows, ((1,), (0,)))
        parts = [scaled[:, :lo]] if lo else []
        parts.append(inverse)
        if hi < RANK:
            parts.append(scaled[:, hi:])
        pivot_rows = jnp.concatenate(parts, axis=1)
        if hi < RANK:
            update = dot(scaled[:, hi:], pivot_rows, ((0,), (0,)))
            below = out_ref[hi:, :]
            cols = lax.broadcasted_iota(jnp.int32, below.shape, 1)
            out_ref[hi:, :] = jnp.where((cols >= lo) & (cols < hi), 0.0, below) - update
        cols = lax.broadcasted_iota(jnp.int32, pivot_rows.shape, 1)
        out_ref[lo:hi, :] = jnp.where(cols < hi, pivot_rows, 0.0)


def orthonormal_right(product_ref, factor_ref, inverse_ref, right_ref):
    step = 2 * RANK
    chunk = lambda ref, c: ref[pl.ds(pl.multiple_of(c * step, step), step), :]
    zero = jnp.zeros((RANK, RANK), jnp.float32)
    add = lambda c, gram: gram + dot(chunk(factor_ref, c), chunk(product_ref, c), ((0,), (0,)))
    inverse_factor(lax.fori_loop(0, KV // step, add, zero), inverse_ref)

    def scale(c, squares):
        right = dot(chunk(product_ref, c), inverse_ref[...], ((1,), (1,)))
        right_ref[pl.ds(pl.multiple_of(c * step, step), step), :] = right
        return squares + jnp.sum(right * right, axis=0, keepdims=True)

    squares = lax.fori_loop(0, KV // step, scale, jnp.zeros((1, RANK), jnp.float32))
    return jnp.sqrt(squares + epsilon)


def next_factor_kernel(product_ref, factor_ref, out_ref, inverse_ref):
    norms = orthonormal_right(product_ref, factor_ref, inverse_ref, out_ref)
    out_ref[...] = out_ref[...] / norms


def last_factor_kernel(col_ref, product_ref, factor_ref, out_ref, inverse_ref, right_ref):
    norms = orthonormal_right(product_ref, factor_ref, inverse_ref, right_ref)
    right = right_ref[pl.ds(pl.multiple_of(col_ref[0] * WIDTH, WIDTH), WIDTH), :]
    factor = right / norms
    scale = math.sqrt(D * KV / RANK)
    stacked = jnp.concatenate([decay_keep * right, scale * factor], axis=0)
    out_ref[:RANK, :] = dot(stacked, inverse_ref[...], ((1,), (0,))).T
    out_ref[RANK:, :] = factor


vmem = pltpu.CompilerParams(vmem_limit_bytes=32 * 2**20)


def next_factor(product, factor):
    return pl.pallas_call(
        next_factor_kernel,
        out_shape=jax.ShapeDtypeStruct((KV, RANK), jnp.float32),
        scratch_shapes=[pltpu.VMEM((RANK, RANK), jnp.float32)],
        compiler_params=vmem,
        name="next_factor",
    )(product, factor)


def last_factor(col, product, factor):
    whole = pl.BlockSpec(memory_space=pltpu.VMEM)
    return pl.pallas_call(
        last_factor_kernel,
        in_specs=[pl.BlockSpec(memory_space=pltpu.SMEM), whole, whole],
        out_shape=jax.ShapeDtypeStruct((RANK + WIDTH, RANK), jnp.float32),
        scratch_shapes=[
            pltpu.VMEM((RANK, RANK), jnp.float32),
            pltpu.VMEM((KV, RANK), jnp.float32),
        ],
        compiler_params=vmem,
        name="last_factor",
    )(col[None], product, factor)


def halves(value):
    high = value.astype(jnp.bfloat16)
    return high, (value - high.astype(jnp.float32)).astype(jnp.bfloat16)


def output_kernel(
    core_ref, left_ref, own_ref, got_ref, momentum_ref, grad_ref,
    momentum_out, update_out, factor_out,
):
    matrix = pl.program_id(0)
    weight = jnp.where(matrix == core_ref[0], own_ref[:RANK, :], got_ref[:RANK, :])
    high, low = halves(weight)
    product = lambda a, b: jnp.dot(a, b, preferred_element_type=jnp.float32)
    rows = left_ref.shape[2]
    for x in range(NX):
        left_high, left_low = halves(left_ref[x, 0])
        both = product(left_low, high) + product(left_high, low) + product(left_high, high)
        here = slice(x * rows, (x + 1) * rows)
        buffer = momentum_ref[0, 0, here] + grad_ref[0, 0, here].astype(jnp.float32)
        momentum_out[0, 0, here] = buffer - both[:, :WIDTH]
        update_out[0, here] = both[:, WIDTH:].astype(jnp.bfloat16)

    @pl.when(matrix == 0)
    def _():
        first = core_ref[0] == 0
        mine, other = own_ref[RANK:, :], got_ref[RANK:, :]
        factor_out[:, 0, :] = jnp.where(first, mine, other)
        factor_out[:, 1, :] = jnp.where(first, other, mine)


def outputs(core, lefts, own, got, momentum, grad):
    rows = momentum.shape[2]
    data = pl.BlockSpec((1, 1, rows, WIDTH), lambda m: (0, m, 0, 0))
    weight = pl.BlockSpec((RANK + WIDTH, RANK), lambda m: (0, 0))
    return pl.pallas_call(
        output_kernel,
        grid=(NC,),
        in_specs=[
            pl.BlockSpec(memory_space=pltpu.SMEM),
            pl.BlockSpec((NX, 1, rows // NX, RANK), lambda m: (0, m, 0, 0)),
            weight,
            weight,
            data,
            data,
        ],
        out_specs=[
            data,
            pl.BlockSpec((1, rows, WIDTH), lambda m: (m, 0, 0)),
            pl.BlockSpec((WIDTH, NC, RANK), lambda m: (0, 0, 0)),
        ],
        out_shape=[
            jax.ShapeDtypeStruct(momentum.shape, jnp.float32),
            jax.ShapeDtypeStruct(momentum.shape[1:], jnp.bfloat16),
            jax.ShapeDtypeStruct((WIDTH, NC, RANK), jnp.float32),
        ],
        compiler_params=pltpu.CompilerParams(vmem_limit_bytes=56 * 2**20),
        name="outputs",
    )(core[None], lefts.reshape(NX, NC, -1, RANK), own, got, momentum, grad)


def ring(size, step):
    return [(k, (k + step) % size) for k in range(size)]


def share_quad(share):
    place = lax.rem(lax.axis_index("col"), QUAD)
    whole = jnp.zeros((QUAD,) + share.shape, share.dtype)
    parts = [(0, share)]
    for d in range(1, QUAD):
        pairs = [(k, k // QUAD * QUAD + (k + d) % QUAD) for k in range(NZ)]
        parts.append((QUAD - d, lax.ppermute(share, "col", pairs)))
    for offset, part in parts:
        whole = lax.dynamic_update_index_in_dim(whole, part, lax.rem(place + offset, QUAD), 0)
    return whole


def sum_over_rows(rows, left):
    place = lax.rem(lax.axis_index("col"), QUAD)
    part = KV // QUAD
    columns = lax.dynamic_slice_in_dim(rows, place * part, part, 1)
    partial = dot(columns, left, ((0,), (0,)))
    share = lax.all_to_all(partial.reshape(NX * NY, -1, RANK), ("x", "row"), 0, 0)
    share = share_quad(jnp.sum(share, axis=0))
    spread = jnp.broadcast_to(share[None], (NX * NY,) + share.shape)
    whole = lax.all_to_all(spread, ("x", "row"), 0, 0)
    return jnp.swapaxes(whole, 0, 1).reshape(KV, RANK)


def gather_rows(grad, momentum):
    core, x, z = (lax.axis_index(name) for name in ("core", "x", "col"))
    pick = lambda array, m: lax.dynamic_index_in_dim(array[0], m, 0, False)
    buffer = lambda m: pick(momentum, m) + pick(grad, m).astype(jnp.float32)

    came = lax.ppermute(buffer(1 - core), "core", [(0, 1), (1, 0)])
    pieces = (buffer(core) + came).reshape(NX, -1, WIDTH)
    piece = lambda d: lax.dynamic_index_in_dim(pieces, lax.rem(x + d, NX), 0, False)
    came = [lax.ppermute(piece(d), "x", ring(NX, d)) for d in (2, 1, 3)]
    block = (piece(0) + came[1] + came[2] + came[0]) / (NX * NC)

    up, down = ring(NZ, 1), ring(NZ, -1)
    below = above = block
    parts = [(0, block)]
    for step in range(1, NZ // 2 + 1):
        below = lax.ppermute(below, "col", up)
        parts.append((NZ - step, below))
        if step < NZ // 2:
            above = lax.ppermute(above, "col", down)
            parts.append((step, above))
    rows = jnp.zeros((block.shape[0], KV), jnp.float32)
    for offset, part in parts:
        rows = lax.dynamic_update_slice(rows, part, (0, lax.rem(z + offset, NZ) * WIDTH))
    return rows


def shards(grad, momentum, right_factor):
    core = lax.axis_index("core")
    own_factor = lax.dynamic_index_in_dim(right_factor, core, 1, False)
    factor = lax.all_gather(own_factor, "col", axis=0, tiled=True)
    rows = gather_rows(grad, momentum)

    for repeat in range(ITERS):
        left = dot(rows, factor, ((1,), (0,)))
        product = sum_over_rows(rows, left)
        if repeat < ITERS - 1:
            factor = next_factor(product, factor)
    lefts = lax.all_gather(left, ("x", "core"), axis=0)

    sent = last_factor(lax.axis_index("col"), product, factor)
    got = lax.ppermute(sent, "core", [(0, 1), (1, 0)])
    return tuple(outputs(core, lefts, sent, got, momentum, grad))


def solution(mesh):
    split = Mesh(mesh.devices.reshape(NX, NC, NY, NZ), ("x", "core", "row", "col"))
    data = P(("x", "core"), None, "row", "col")
    return jax.shard_map(
        shards,
        mesh=split,
        in_specs=(data, data, P("col", None, None)),
        out_specs=(data, P(None, "row", "col"), P("col", None, None)),
        check_vma=False,
    )
```

profile of v0, /device:TPU:1, one launch (start us, length us, event | category | flops | bytes accessed | tf_op | source)
XLA Modules:
  0.0 203.6 jit_solution(17777820527770038464)
XLA Ops:
  7.2 0.0 copy-start
  7.2 0.0 copy-start.3
  7.2 0.0 all-gather.5.cloned.1.call-start
  7.2 1.6 add_bitcast_fusion
  8.8 3.3 %collective-permute-start = (f32[2048,128]{1,0:T(8,128)S(1)}, f32[2048,128]{1,0:T(8,128)}, u32[]{:S(2)}, u32[]{:S(2)}) collective-permute-start(f32[2048,128]{1,0:T(8,128)S(1)} %add_bitcast_fusion), channel_id=1, source_target_pairs={{0,32},{32,0},{1,33},{33,1},{2,34},{34,2},{3,35},{35,3},{4,36},{36... | collective-permute-start | bytes 3145736 | tf_op jit(solution)/shard_map/ppermute | solution.py:244
  12.2 2.4 %collective-permute-done = f32[2048,128]{1,0:T(8,128)} collective-permute-done((f32[2048,128]{1,0:T(8,128)S(1)}, f32[2048,128]{1,0:T(8,128)}, u32[]{:S(2)}, u32[]{:S(2)}) %collective-permute-start) | collective-permute-done | bytes 1048608 | tf_op jit(solution)/shard_map/ppermute | solution.py:244
  14.6 1.5 bitcast_add_fusion
  16.1 0.1 dynamic-slice_bitcast_fusion.2
  16.2 0.1 collective-permute-start.1
  16.2 1.9 collective-permute-start.3
  18.2 1.2 collective-permute-start.2
  19.3 0.1 constant_dynamic-slice_fusion
  19.4 0.7 copy.10
  20.1 0.0 all-gather.5.cloned.1.call-update
  20.1 5.6 %collective-permute-done.1 = f32[512,128]{1,0:T(8,128)S(1)} collective-permute-done((f32[512,128]{1,0:T(8,128)S(1)}, f32[512,128]{1,0:T(8,128)S(1)}, u32[]{:S(2)}, u32[]{:S(2)}) %collective-permute-start.1) | collective-permute-done | bytes 262176 | tf_op jit(solution)/shard_map/ppermute | solution.py:247
  25.7 4.2 %collective-permute-done.3 = f32[512,128]{1,0:T(8,128)S(1)} collective-permute-done((f32[512,128]{1,0:T(8,128)S(1)}, f32[512,128]{1,0:T(8,128)S(1)}, u32[]{:S(2)}, u32[]{:S(2)}) %collective-permute-start.3) | collective-permute-done | bytes 262176 | tf_op jit(solution)/shard_map/ppermute | solution.py:247
  29.9 0.7 copy-done.7
  30.6 0.4 collective-permute-done.2
  31.0 0.2 broadcast_in_dim.49
  31.2 0.7 copy-done.6
  31.9 0.1 copy-done.8
  32.0 1.0 constant_dynamic-update-slice_fusion.7
  33.0 1.3 collective-permute-start.4
  34.3 4.0 %collective-permute-start.5 = (f32[512,128]{1,0:T(8,128)S(1)}, f32[512,128]{1,0:T(8,128)S(1)}, u32[]{:S(2)}, u32[]{:S(2)}) collective-permute-start(f32[512,128]{1,0:T(8,128)S(1)} %get-tuple-element.4), channel_id=1, source_target_pairs={{0,7},{1,0},{2,1},{3,2},{4,3},{5,4},{6,5},{7,6},{8,15},{9,8},{10,9... | collective-permute-start | bytes 786440 | tf_op jit(solution)/shard_map/ppermute | solution.py:257
  38.3 9.5 %collective-permute-done.4 = f32[512,128]{1,0:T(8,128)S(1)} collective-permute-done((f32[512,128]{1,0:T(8,128)S(1)}, f32[512,128]{1,0:T(8,128)S(1)}, u32[]{:S(2)}, u32[]{:S(2)}) %collective-permute-start.4) | collective-permute-done | bytes 262176 | tf_op jit(solution)/shard_map/ppermute | solution.py:254
  47.8 2.7 %collective-permute-start.7 = (f32[512,128]{1,0:T(8,128)S(1)}, f32[512,128]{1,0:T(8,128)S(1)}, u32[]{:S(2)}, u32[]{:S(2)}) collective-permute-start(f32[512,128]{1,0:T(8,128)S(1)} %collective-permute-done.5), channel_id=1, source_target_pairs={{0,7},{1,0},{2,1},{3,2},{4,3},{5,4},{6,5},{7,6},{8,15},{9,8},{10,9... | collective-permute-start | bytes 786440 | tf_op jit(solution)/shard_map/ppermute | solution.py:257
  50.5 8.5 %collective-permute-done.6 = f32[512,128]{1,0:T(8,128)S(1)} collective-permute-done((f32[512,128]{1,0:T(8,128)S(1)}, f32[512,128]{1,0:T(8,128)S(1)}, u32[]{:S(2)}, u32[]{:S(2)}) %collective-permute-start.6) | collective-permute-done | bytes 262176 | tf_op jit(solution)/shard_map/ppermute | solution.py:254
  58.9 0.0 collective-permute-start.8
  59.0 0.0 collective-permute-done.7
  59.0 2.7 %collective-permute-start.9 = (f32[512,128]{1,0:T(8,128)S(1)}, f32[512,128]{1,0:T(8,128)S(1)}, u32[]{:S(2)}, u32[]{:S(2)}) collective-permute-start(f32[512,128]{1,0:T(8,128)S(1)} %collective-permute-done.7), channel_id=1, source_target_pairs={{0,7},{1,0},{2,1},{3,2},{4,3},{5,4},{6,5},{7,6},{8,15},{9,8},{10,9... | collective-permute-start | bytes 786440 | tf_op jit(solution)/shard_map/ppermute | solution.py:257
  61.8 4.5 %collective-permute-done.8 = f32[512,128]{1,0:T(8,128)S(1)} collective-permute-done((f32[512,128]{1,0:T(8,128)S(1)}, f32[512,128]{1,0:T(8,128)S(1)}, u32[]{:S(2)}, u32[]{:S(2)}) %collective-permute-start.8) | collective-permute-done | bytes 262176 | tf_op jit(solution)/shard_map/ppermute | solution.py:254
  66.3 0.0 collective-permute-start.10
  66.4 0.0 collective-permute-done.9
  66.4 6.3 %collective-permute-done.10 = f32[512,128]{1,0:T(8,128)S(1)} collective-permute-done((f32[512,128]{1,0:T(8,128)S(1)}, f32[512,128]{1,0:T(8,128)S(1)}, u32[]{:S(2)}, u32[]{:S(2)}) %collective-permute-start.10) | collective-permute-done | bytes 262176 | tf_op jit(solution)/shard_map/ppermute | solution.py:254
  72.8 0.0 all-gather.5.cloned.1.call-done
  72.8 3.0 %fusion.9 = f32[512,256]{1,0:T(8,128)S(1)} fusion(f32[512,1024]{1,0:T(8,128)S(1)} %constant_dynamic-update-slice_fusion, f32[1024,1,256]{2,0,1:T(8,128)} %all-gather.5.cloned.1.call-done), kind=kOutput, calls=%fused_computation.32 | convolution fusion | flops 1610612736 | bytes 3670016 | tf_op jit(solution)/shard_map/dot_general | solution.py:25
  75.9 1.7 fusion.2
  77.6 6.3 %all-to-all-start = ((f32[16,16,256]{2,1,0:T(8,128)}), f32[16,16,256]{2,1,0:T(8,128)S(1)}, u32[]{:S(2)}, u32[]{:S(2)}) async-start(f32[16,16,256]{2,1,0:T(8,128)} %bitcast.9), calls=%async_computation | async-start | bytes 524288 | tf_op jit(solution)/shard_map/all_to_all | solution.py:232
  83.9 0.0 all-gather.7.cloned.1.call-start
  84.0 7.2 %all-to-all-done = f32[16,16,256]{2,1,0:T(8,128)S(1)} async-done(((f32[16,16,256]{2,1,0:T(8,128)}), f32[16,16,256]{2,1,0:T(8,128)S(1)}, u32[]{:S(2)}, u32[]{:S(2)}) %all-to-all-start) | async-done | bytes 262176 | tf_op jit(solution)/shard_map/all_to_all | solution.py:232
  91.3 0.6 collective-permute-start.13
  91.9 0.0 collective-permute-start.12
  91.9 0.9 collective-permute-start.11
  92.8 3.5 %collective-permute-done.11 = f32[16,256]{1,0:T(8,128)S(1)} collective-permute-done((f32[16,256]{1,0:T(8,128)S(1)}, f32[16,256]{1,0:T(8,128)S(1)}, u32[]{:S(2)}, u32[]{:S(2)}) %collective-permute-start.11) | collective-permute-done | bytes 16416 | tf_op jit(solution)/shard_map/ppermute | solution.py:221
  96.3 0.0 collective-permute-done.13
  96.3 0.1 broadcast_in_dim.55
  96.5 15.2 %all_to_all.20 = f32[16,4,16,256]{3,2,1,0:T(8,128)S(1)} all-to-all(f32[16,4,16,256]{3,2,1,0:T(8,128)S(1)} %broadcast_in_dim.55), channel_id=1, replica_groups=mesh['x'=4,'core'=2,'row'=4,'col'=8] {'x','row'}, dimensions={0} | all-to-all | bytes 2097152 | tf_op jit(solution)/shard_map/all_to_all | solution.py:235
  111.6 0.1 copy.8
  111.7 11.8 %next_factor.1.factor_ref = f32[1024,256]{1,0:T(8,128)S(1)} custom-call(f32[1024,256]{1,0:T(8,128)S(1)} %bitcast.54, f32[1024,256]{1,0:T(8,128)S(1)} %bitcast.53), custom_call_target="tpu_custom_call" | custom-call | tf_op jit(solution)/shard_map/next_factor/pallas_call | solution.py:127
  123.6 2.6 %fusion.12 = f32[512,256]{1,0:T(8,128)} fusion(f32[512,1024]{1,0:T(8,128)S(1)} %constant_dynamic-update-slice_fusion, f32[1024,256]{1,0:T(8,128)S(1)} %next_factor.1.factor_ref), kind=kOutput, calls=%fused_computation.34 | convolution fusion | flops 1610612736 | bytes 3670016 | tf_op jit(solution)/shard_map/dot_general | solution.py:25
  126.2 0.0 all-gather.7.cloned.1.call-update
  126.2 2.1 %fusion = f32[256,256]{1,0:T(8,128)S(1)} fusion(f32[512,256]{1,0:T(8,128)} %fusion.12, f32[512,1024]{1,0:T(8,128)S(1)} %constant_dynamic-update-slice_fusion, s32[]{:T(128)S(6)} %select_n.84), kind=kOutput, calls=%fused_computation.2 | convolution fusion | flops 402653184 | bytes 1310724 | tf_op jit(solution)/shard_map/dot_general | solution.py:25
  128.2 10.2 %all_to_all.22 = f32[16,16,256]{2,1,0:T(8,128)S(1)} all-to-all(f32[16,16,256]{2,1,0:T(8,128)S(1)} %bitcast.61), channel_id=1, replica_groups=mesh['x'=4,'core'=2,'row'=4,'col'=8] {'x','row'}, dimensions={0} | all-to-all | bytes 524288 | tf_op jit(solution)/shard_map/all_to_all | solution.py:232
  138.4 1.3 collective-permute-start.16
  139.7 0.8 collective-permute-start.14
  140.6 3.8 %collective-permute-done.14 = f32[16,256]{1,0:T(8,128)S(1)} collective-permute-done((f32[16,256]{1,0:T(8,128)S(1)}, f32[16,256]{1,0:T(8,128)S(1)}, u32[]{:S(2)}, u32[]{:S(2)}) %collective-permute-start.14) | collective-permute-done | bytes 16416 | tf_op jit(solution)/shard_map/ppermute | solution.py:221
  144.4 0.1 broadcast_in_dim.61
  144.5 25.0 %all_to_all.21 = f32[16,4,16,256]{3,2,1,0:T(8,128)S(1)} all-to-all(f32[16,4,16,256]{3,2,1,0:T(8,128)S(1)} %broadcast_in_dim.61), channel_id=1, replica_groups=mesh['x'=4,'core'=2,'row'=4,'col'=8] {'x','row'}, dimensions={0} | all-to-all | bytes 2097152 | tf_op jit(solution)/shard_map/all_to_all | solution.py:235
  169.5 0.1 copy.9
  169.6 12.2 %last_factor.1.own_ref = f32[384,256]{1,0:T(8,128)S(1)} custom-call(s32[1]{0:T(128)} %bitcast.17.col_ref, f32[1024,256]{1,0:T(8,128)S(1)} %bitcast.55, f32[1024,256]{1,0:T(8,128)S(1)} %next_factor.1.factor_ref), custom_call_target="tpu_custom_call" | custom-call | tf_op jit(solution)/shard_map/last_factor/pallas_call | solution.py:138
  181.8 7.3 %collective-permute-start.17 = (f32[384,256]{1,0:T(8,128)S(1)}, f32[384,256]{1,0:T(8,128)S(1)}, u32[]{:S(2)}, u32[]{:S(2)}) collective-permute-start(f32[384,256]{1,0:T(8,128)S(1)} %last_factor.1.own_ref), channel_id=1, source_target_pairs={{0,32},{32,0},{1,33},{33,1},{2,34},{34,2},{3,35},{35,3},{4,36},{36... | collective-permute-start | bytes 1179656 | tf_op jit(solution)/shard_map/ppermute | solution.py:279
  189.1 1.3 collective-permute-done.17.got_ref
  190.5 0.7 copy-done.4
  191.2 5.6 %outputs.1 = (f32[1,2,2048,128]{3,2,1,0:T(8,128)}, bf16[2,2048,128]{2,1,0:T(8,128)(2,1)}, f32[128,2,256]{2,1,0:T(2,128)}) custom-call(s32[1]{0:T(128)} %bitcast.core_ref, f32[4,2,512,256]{3,2,1,0:T(8,128)} %bitcast.56, f32[384,256]{1,0:T(8,128)} %copy-done.2, f32[384,256]{1,0:T(8,128)} %copy-done.4, f32[1,2,2048,128]{3,2,1,0:T(8,128)} %momentum_ref.1, ...), custom_call_target="tpu_custom_call" | custom-call | tf_op jit(solution)/shard_map/outputs/pallas_call | solution.py:185
  (38 shorter events, 0.3 us)
Async XLA Ops:
  7.2 12.2 %copy-start = (f32[128,2,256]{2,1,0:T(2,128)S(1)}, f32[128,2,256]{2,1,0:T(2,128)}, u32[]{:S(2)}) copy-start(f32[128,2,256]{2,1,0:T(2,128)} %param.5) | copy-start | bytes 786436
  7.2 7.4 %copy-start.3 = (f32[1,2,2048,128]{3,2,1,0:T(8,128)S(1)}, f32[1,2,2048,128]{3,2,1,0:T(8,128)}, u32[]{:S(2)}) copy-start(f32[1,2,2048,128]{3,2,1,0:T(8,128)} %momentum_ref.1) | copy-start | bytes 6291460
  7.2 65.6 %all-gather.5.cloned.1.call-start = ((), (), s32[]{:S(2)}) async-start(), calls=%async_computation.4 | async-start | bytes 1179648 | tf_op jit(solution)/shard_map/all_gather | solution.py:268
  8.8 5.7 %collective-permute-start = (f32[2048,128]{1,0:T(8,128)S(1)}, f32[2048,128]{1,0:T(8,128)}, u32[]{:S(2)}, u32[]{:S(2)}) collective-permute-start(f32[2048,128]{1,0:T(8,128)S(1)} %add_bitcast_fusion), channel_id=1, source_target_pairs={{0,32},{32,0},{1,33},{33,1},{2,34},{34,2},{3,35},{35,3},{4,36},{36... | collective-permute-start | bytes 3145736 | tf_op jit(solution)/shard_map/ppermute | solution.py:244
  16.2 9.5 %collective-permute-start.1 = (f32[512,128]{1,0:T(8,128)S(1)}, f32[512,128]{1,0:T(8,128)S(1)}, u32[]{:S(2)}, u32[]{:S(2)}) collective-permute-start(f32[512,128]{1,0:T(8,128)S(1)} %get-tuple-element.5), channel_id=1, source_target_pairs={{0,64},{64,128},{128,192},{192,0},{1,65},{65,129},{129,193},{193,1... | collective-permute-start | bytes 786440 | tf_op jit(solution)/shard_map/ppermute | solution.py:247
  16.2 13.6 %collective-permute-start.3 = (f32[512,128]{1,0:T(8,128)S(1)}, f32[512,128]{1,0:T(8,128)S(1)}, u32[]{:S(2)}, u32[]{:S(2)}) collective-permute-start(f32[512,128]{1,0:T(8,128)S(1)} %get-tuple-element.6), channel_id=1, source_target_pairs={{0,128},{64,192},{128,0},{192,64},{1,129},{65,193},{129,1},{193,65... | collective-permute-start | bytes 786440 | tf_op jit(solution)/shard_map/ppermute | solution.py:247
  18.2 12.8 %collective-permute-start.2 = (f32[512,128]{1,0:T(8,128)S(1)}, f32[512,128]{1,0:T(8,128)}, u32[]{:S(2)}, u32[]{:S(2)}) collective-permute-start(f32[512,128]{1,0:T(8,128)S(1)} %get-tuple-element.7), channel_id=1, source_target_pairs={{0,192},{64,0},{128,64},{192,128},{1,193},{65,1},{129,65},{193,129... | collective-permute-start | bytes 786440 | tf_op jit(solution)/shard_map/ppermute | solution.py:247
  25.7 4.2 %copy-start.5 = (f32[512,128]{1,0:T(8,128)}, f32[512,128]{1,0:T(8,128)S(1)}, u32[]{:S(2)}) copy-start(f32[512,128]{1,0:T(8,128)S(1)} %collective-permute-done.1) | copy-start | bytes 786436
  29.9 0.7 copy-start.7
  31.0 1.0 copy-start.6
  31.0 1.0 copy-start.8
  33.0 14.7 %collective-permute-start.4 = (f32[512,128]{1,0:T(8,128)S(1)}, f32[512,128]{1,0:T(8,128)S(1)}, u32[]{:S(2)}, u32[]{:S(2)}) collective-permute-start(f32[512,128]{1,0:T(8,128)S(1)} %get-tuple-element.4), channel_id=1, source_target_pairs={{0,1},{1,2},{2,3},{3,4},{4,5},{5,6},{6,7},{7,0},{8,9},{9,10},{10,1... | collective-permute-start | bytes 786440 | tf_op jit(solution)/shard_map/ppermute | solution.py:254
  34.3 13.5 %collective-permute-start.5 = (f32[512,128]{1,0:T(8,128)S(1)}, f32[512,128]{1,0:T(8,128)S(1)}, u32[]{:S(2)}, u32[]{:S(2)}) collective-permute-start(f32[512,128]{1,0:T(8,128)S(1)} %get-tuple-element.4), channel_id=1, source_target_pairs={{0,7},{1,0},{2,1},{3,2},{4,3},{5,4},{6,5},{7,6},{8,15},{9,8},{10,9... | collective-permute-start | bytes 786440 | tf_op jit(solution)/shard_map/ppermute | solution.py:257
  47.8 11.2 %collective-permute-start.6 = (f32[512,128]{1,0:T(8,128)S(1)}, f32[512,128]{1,0:T(8,128)S(1)}, u32[]{:S(2)}, u32[]{:S(2)}) collective-permute-start(f32[512,128]{1,0:T(8,128)S(1)} %collective-permute-done.4), channel_id=1, source_target_pairs={{0,1},{1,2},{2,3},{3,4},{4,5},{5,6},{6,7},{7,0},{8,9},{9,10},{10,1... | collective-permute-start | bytes 786440 | tf_op jit(solution)/shard_map/ppermute | solution.py:254
  47.8 11.2 %collective-permute-start.7 = (f32[512,128]{1,0:T(8,128)S(1)}, f32[512,128]{1,0:T(8,128)S(1)}, u32[]{:S(2)}, u32[]{:S(2)}) collective-permute-start(f32[512,128]{1,0:T(8,128)S(1)} %collective-permute-done.5), channel_id=1, source_target_pairs={{0,7},{1,0},{2,1},{3,2},{4,3},{5,4},{6,5},{7,6},{8,15},{9,8},{10,9... | collective-permute-start | bytes 786440 | tf_op jit(solution)/shard_map/ppermute | solution.py:257
  58.9 7.4 %collective-permute-start.8 = (f32[512,128]{1,0:T(8,128)S(1)}, f32[512,128]{1,0:T(8,128)S(1)}, u32[]{:S(2)}, u32[]{:S(2)}) collective-permute-start(f32[512,128]{1,0:T(8,128)S(1)} %collective-permute-done.6), channel_id=1, source_target_pairs={{0,1},{1,2},{2,3},{3,4},{4,5},{5,6},{6,7},{7,0},{8,9},{9,10},{10,1... | collective-permute-start | bytes 786440 | tf_op jit(solution)/shard_map/ppermute | solution.py:254
  59.0 7.4 %collective-permute-start.9 = (f32[512,128]{1,0:T(8,128)S(1)}, f32[512,128]{1,0:T(8,128)S(1)}, u32[]{:S(2)}, u32[]{:S(2)}) collective-permute-start(f32[512,128]{1,0:T(8,128)S(1)} %collective-permute-done.7), channel_id=1, source_target_pairs={{0,7},{1,0},{2,1},{3,2},{4,3},{5,4},{6,5},{7,6},{8,15},{9,8},{10,9... | collective-permute-start | bytes 786440 | tf_op jit(solution)/shard_map/ppermute | solution.py:257
  66.3 6.4 %collective-permute-start.10 = (f32[512,128]{1,0:T(8,128)S(1)}, f32[512,128]{1,0:T(8,128)S(1)}, u32[]{:S(2)}, u32[]{:S(2)}) collective-permute-start(f32[512,128]{1,0:T(8,128)S(1)} %collective-permute-done.8), channel_id=1, source_target_pairs={{0,1},{1,2},{2,3},{3,4},{4,5},{5,6},{6,7},{7,0},{8,9},{9,10},{10,1... | collective-permute-start | bytes 786440 | tf_op jit(solution)/shard_map/ppermute | solution.py:254
  77.6 13.6 %all-to-all-start = ((f32[16,16,256]{2,1,0:T(8,128)}), f32[16,16,256]{2,1,0:T(8,128)S(1)}, u32[]{:S(2)}, u32[]{:S(2)}) async-start(f32[16,16,256]{2,1,0:T(8,128)} %bitcast.9), calls=%async_computation | async-start | bytes 524288 | tf_op jit(solution)/shard_map/all_to_all | solution.py:232
  83.9 106.5 %all-gather.7.cloned.1.call-start = ((), (), s32[]{:S(2)}) async-start(), calls=%async_computation.5 | async-start | bytes 4718592 | tf_op jit(solution)/shard_map/all_gather | solution.py:276
  91.3 5.0 %collective-permute-start.13 = (f32[16,256]{1,0:T(8,128)S(1)}, f32[16,256]{1,0:T(8,128)S(1)}, u32[]{:S(2)}, u32[]{:S(2)}) collective-permute-start(f32[16,256]{1,0:T(8,128)S(1)} %reduce_sum.18), channel_id=1, source_target_pairs={{0,3},{1,0},{2,1},{3,2},{4,7},{5,4},{6,5},{7,6},{8,11},{9,8},{10,9... | collective-permute-start | bytes 49160 | tf_op jit(solution)/shard_map/ppermute | solution.py:221
  91.9 4.4 %collective-permute-start.12 = (f32[16,256]{1,0:T(8,128)S(1)}, f32[16,256]{1,0:T(8,128)S(1)}, u32[]{:S(2)}, u32[]{:S(2)}) collective-permute-start(f32[16,256]{1,0:T(8,128)S(1)} %reduce_sum.18), channel_id=1, source_target_pairs={{0,2},{1,3},{2,0},{3,1},{4,6},{5,7},{6,4},{7,5},{8,10},{9,11},{10,... | collective-permute-start | bytes 49160 | tf_op jit(solution)/shard_map/ppermute | solution.py:221
  91.9 4.4 %collective-permute-start.11 = (f32[16,256]{1,0:T(8,128)S(1)}, f32[16,256]{1,0:T(8,128)S(1)}, u32[]{:S(2)}, u32[]{:S(2)}) collective-permute-start(f32[16,256]{1,0:T(8,128)S(1)} %reduce_sum.18), channel_id=1, source_target_pairs={{0,1},{1,2},{2,3},{3,0},{4,5},{5,6},{6,7},{7,4},{8,9},{9,10},{10,1... | collective-permute-start | bytes 49160 | tf_op jit(solution)/shard_map/ppermute | solution.py:221
  96.4 15.3 %copy-start.1 = (f32[1024,1,256]{2,0,1:T(8,128)S(1)}, f32[1024,1,256]{2,0,1:T(8,128)}, u32[]{:S(2)}) copy-start(f32[1024,1,256]{2,0,1:T(8,128)} %all-gather.5.cloned.1.call-done) | copy-start | bytes 3145732
  138.4 5.9 %collective-permute-start.16 = (f32[16,256]{1,0:T(8,128)S(1)}, f32[16,256]{1,0:T(8,128)S(1)}, u32[]{:S(2)}, u32[]{:S(2)}) collective-permute-start(f32[16,256]{1,0:T(8,128)S(1)} %reduce_sum.19), channel_id=1, source_target_pairs={{0,3},{1,0},{2,1},{3,2},{4,7},{5,4},{6,5},{7,6},{8,11},{9,8},{10,9... | collective-permute-start | bytes 49160 | tf_op jit(solution)/shard_map/ppermute | solution.py:221
  139.7 4.6 %collective-permute-start.15 = (f32[16,256]{1,0:T(8,128)S(1)}, f32[16,256]{1,0:T(8,128)S(1)}, u32[]{:S(2)}, u32[]{:S(2)}) collective-permute-start(f32[16,256]{1,0:T(8,128)S(1)} %reduce_sum.19), channel_id=1, source_target_pairs={{0,2},{1,3},{2,0},{3,1},{4,6},{5,7},{6,4},{7,5},{8,10},{9,11},{10,... | collective-permute-start | bytes 49160 | tf_op jit(solution)/shard_map/ppermute | solution.py:221
  139.7 4.6 %collective-permute-start.14 = (f32[16,256]{1,0:T(8,128)S(1)}, f32[16,256]{1,0:T(8,128)S(1)}, u32[]{:S(2)}, u32[]{:S(2)}) collective-permute-start(f32[16,256]{1,0:T(8,128)S(1)} %reduce_sum.19), channel_id=1, source_target_pairs={{0,1},{1,2},{2,3},{3,0},{4,5},{5,6},{6,7},{7,4},{8,9},{9,10},{10,1... | collective-permute-start | bytes 49160 | tf_op jit(solution)/shard_map/ppermute | solution.py:221
  181.8 8.7 %copy-start.2 = (f32[384,256]{1,0:T(8,128)}, f32[384,256]{1,0:T(8,128)S(1)}, u32[]{:S(2)}) copy-start(f32[384,256]{1,0:T(8,128)S(1)} %last_factor.1.own_ref) | copy-start | bytes 1179652
  181.8 8.7 %collective-permute-start.17 = (f32[384,256]{1,0:T(8,128)S(1)}, f32[384,256]{1,0:T(8,128)S(1)}, u32[]{:S(2)}, u32[]{:S(2)}) collective-permute-start(f32[384,256]{1,0:T(8,128)S(1)} %last_factor.1.own_ref), channel_id=1, source_target_pairs={{0,32},{32,0},{1,33},{33,1},{2,34},{34,2},{3,35},{35,3},{4,36},{36... | collective-permute-start | bytes 1179656 | tf_op jit(solution)/shard_map/ppermute | solution.py:279
  190.4 0.8 copy-start.4
Sparse Core Ops, SparseCore 0:
  20.2 37.1 all-gather.4
  126.3 47.1 all-gather.6
where the time goes:
time: 204 us
  waiting for transfers between devices  57.2 us (28%)
  blocking collectives  50.4 us (25%)
  starting transfers between devices  34.6 us (17%)
  Pallas kernels  29.6 us (15%)
  between operations  14.4 us (7%)
  matrix products  9.41 us (5%)
  other arithmetic  4.16 us (2%)
  local copies, waits for them, and re-layouts  3.97 us (2%)
    all_to_all x2, blocking collectives, sum_over_rows(): whole = lax.all_to_all(spread, ('x', 'row'), 0, 0)  40.2 us
    ppermute x4, waiting for transfers between devices, gather_rows(): below = lax.ppermute(below, 'col', up)  28.8 us
    pallas_call x1, Pallas kernels, last_factor(): pl.pallas_call(last_factor_kernel, in_specs=[pl.BlockSpec(memory_space=pl...  12.2 us
    pallas_call x1, Pallas kernels, next_factor(): pl.pallas_call(next_factor_kernel, out_shape=jax.ShapeDtypeStruct((KV, RA...  11.8 us
    all_to_all x1, blocking collectives, sum_over_rows(): lax.all_to_all(partial.reshape(NX * NY, -1, RANK), ('x', 'row'), 0, 0)  10.2 us
    ppermute x3, waiting for transfers between devices, gather_rows(): came = [lax.ppermute(piece(d), 'x', ring(NX, d)) for d in (2, 1, 3)]  10.1 us
    ppermute x3, starting transfers between devices, gather_rows(): above = lax.ppermute(above, 'col', down)  9.45 us
    dot_general x4, matrix products, dot(): lax.dot_general(a, b, (contract, ((), ())), precision=highest, preferred_...  9.41 us
  transfers between devices with their start and end apart: 21, of which 12 were waited for; matrix products, arithmetic and copies ran while one was open for 2% of the time, Pallas kernels for 6%

commit v1 on v0

--- a/solution.py
+++ b/solution.py
@@ -12,7 +12,9 @@
 RANK = 256
 ITERS = 2
 NX, NC, NY, NZ = 4, 2, 4, 8
+COL = ("quad", "place")
 BLOCK = 64
+PANEL = 16
 QUAD = 4
 WIDTH = KV // NZ
 
@@ -33,35 +35,33 @@
     chunks = [block[8 * c : 8 * c + 8] for c in range(count)]
     sub = lax.broadcasted_iota(jnp.int32, (8, size), 0)
     lane = lax.broadcasted_iota(jnp.int32, (8, size), 1)
-    pivots = []
-    for p in range(count):
-        lo = 8 * p
+    pivots = [None] * count
+    for lo in range(0, size, PANEL):
         spread = {}
-        for c in range(p, count):
-            for k in range(8):
+        for c in range(lo // 8, count):
+            for k in range(PANEL):
                 spread[k, c] = jnp.broadcast_to(chunks[c][:, lo + k : lo + k + 1], (8, size))
-        panel = (lane >= lo) & (lane < lo + 8)
-        for c in range(p, count):
-            unit = jnp.where(lane == sub + lo, 1.0, 0.0) if c == p else 0.0
+        panel = (lane >= lo) & (lane < lo + PANEL)
+        for c in range(lo // 8, count):
+            unit = jnp.where(lane == sub + 8 * c, 1.0, 0.0) if 8 * c < lo + PANEL else 0.0
             chunks[c] = jnp.where(panel, unit, chunks[c])
-        held = None
-        for j in range(8):
-            pivot = jnp.broadcast_to(spread[j, p][j : j + 1, :], (8, size))
-            held = pivot if held is None else jnp.where(sub >= j, pivot, held)
+        for j in range(PANEL):
+            p, row = divmod(lo + j, 8)
+            pivot = jnp.broadcast_to(spread[j, p][row : row + 1, :], (8, size))
+            pivots[p] = jnp.where(sub >= row, pivot, pivot if row == 0 else pivots[p])
             scale = pltpu.reciprocal(pivot, approx=True)
-            row = jnp.broadcast_to(chunks[p][j : j + 1, :], (8, size)) * scale
+            head = jnp.broadcast_to(chunks[p][row : row + 1, :], (8, size)) * scale
             heads = {
-                k: jnp.broadcast_to(spread[k, p][j : j + 1, :], (8, size)) * scale
-                for k in range(j + 1, 8)
+                k: jnp.broadcast_to(spread[k, p][row : row + 1, :], (8, size)) * scale
+                for k in range(j + 1, PANEL)
             }
             for c in range(p, count):
                 column = spread[j, c]
                 if c == p:
-                    column = jnp.where(sub > j, column, 0.0)
-                chunks[c] = chunks[c] - column * row
+                    column = jnp.where(sub > row, column, 0.0)
+                chunks[c] = chunks[c] - column * head
                 for k in heads:
                     spread[k, c] = spread[k, c] - column * heads[k]
-        pivots.append(held)
     inverse = jnp.concatenate([c * lax.rsqrt(d) for c, d in zip(chunks, pivots)], axis=0)
     row_ids = lax.broadcasted_iota(jnp.int32, (size, size), 0)
     col_ids = lax.broadcasted_iota(jnp.int32, (size, size), 1)
@@ -213,31 +213,39 @@
 
 
 def share_quad(share):
-    place = lax.rem(lax.axis_index("col"), QUAD)
+    place = lax.rem(lax.axis_index(COL), QUAD)
     whole = jnp.zeros((QUAD,) + share.shape, share.dtype)
     parts = [(0, share)]
     for d in range(1, QUAD):
         pairs = [(k, k // QUAD * QUAD + (k + d) % QUAD) for k in range(NZ)]
-        parts.append((QUAD - d, lax.ppermute(share, "col", pairs)))
+        parts.append((QUAD - d, lax.ppermute(share, COL, pairs)))
     for offset, part in parts:
         whole = lax.dynamic_update_index_in_dim(whole, part, lax.rem(place + offset, QUAD), 0)
     return whole
 
 
-def sum_over_rows(rows, left):
-    place = lax.rem(lax.axis_index("col"), QUAD)
+def spread(share, axes, size):
+    return lax.all_to_all(jnp.broadcast_to(share[None], (size,) + share.shape), axes, 0, 0)
+
+
+def sum_over_rows(rows, left, by_row):
+    place = lax.rem(lax.axis_index(COL), QUAD)
     part = KV // QUAD
     columns = lax.dynamic_slice_in_dim(rows, place * part, part, 1)
     partial = dot(columns, left, ((0,), (0,)))
     share = lax.all_to_all(partial.reshape(NX * NY, -1, RANK), ("x", "row"), 0, 0)
-    share = share_quad(jnp.sum(share, axis=0))
-    spread = jnp.broadcast_to(share[None], (NX * NY,) + share.shape)
-    whole = lax.all_to_all(spread, ("x", "row"), 0, 0)
-    return jnp.swapaxes(whole, 0, 1).reshape(KV, RANK)
+    share = jnp.sum(share, axis=0)
+    if not by_row:
+        share = share_quad(share)
+        whole = spread(share, ("x", "row"), NX * NY)
+        return jnp.swapaxes(whole, 0, 1).reshape(KV, RANK)
+    share = spread(share, ("x", "place"), NX * QUAD)
+    whole = spread(share, "row", NY).reshape(NY, NX, QUAD, -1, RANK)
+    return whole.transpose(2, 1, 0, 3, 4).reshape(KV, RANK)
 
 
 def gather_rows(grad, momentum):
-    core, x, z = (lax.axis_index(name) for name in ("core", "x", "col"))
+    core, x, z = (lax.axis_index(name) for name in ("core", "x", COL))
     pick = lambda array, m: lax.dynamic_index_in_dim(array[0], m, 0, False)
     buffer = lambda m: pick(momentum, m) + pick(grad, m).astype(jnp.float32)
 
@@ -251,10 +259,10 @@
     below = above = block
     parts = [(0, block)]
     for step in range(1, NZ // 2 + 1):
-        below = lax.ppermute(below, "col", up)
+        below = lax.ppermute(below, COL, up)
         parts.append((NZ - step, below))
         if step < NZ // 2:
-            above = lax.ppermute(above, "col", down)
+            above = lax.ppermute(above, COL, down)
             parts.append((step, above))
     rows = jnp.zeros((block.shape[0], KV), jnp.float32)
     for offset, part in parts:
@@ -265,28 +273,29 @@
 def shards(grad, momentum, right_factor):
     core = lax.axis_index("core")
     own_factor = lax.dynamic_index_in_dim(right_factor, core, 1, False)
-    factor = lax.all_gather(own_factor, "col", axis=0, tiled=True)
+    factor = lax.all_gather(own_factor, COL, axis=0, tiled=True)
     rows = gather_rows(grad, momentum)
 
     for repeat in range(ITERS):
         left = dot(rows, factor, ((1,), (0,)))
-        product = sum_over_rows(rows, left)
+        product = sum_over_rows(rows, left, by_row=repeat == ITERS - 1)
         if repeat < ITERS - 1:
             factor = next_factor(product, factor)
     lefts = lax.all_gather(left, ("x", "core"), axis=0)
 
-    sent = last_factor(lax.axis_index("col"), product, factor)
+    sent = last_factor(lax.axis_index(COL), product, factor)
     got = lax.ppermute(sent, "core", [(0, 1), (1, 0)])
     return tuple(outputs(core, lefts, sent, got, momentum, grad))
 
 
 def solution(mesh):
-    split = Mesh(mesh.devices.reshape(NX, NC, NY, NZ), ("x", "core", "row", "col"))
-    data = P(("x", "core"), None, "row", "col")
+    shape = (NX, NC, NY, NZ // QUAD, QUAD)
+    split = Mesh(mesh.devices.reshape(shape), ("x", "core", "row") + COL)
+    data = P(("x", "core"), None, "row", COL)
     return jax.shard_map(
         shards,
         mesh=split,
-        in_specs=(data, data, P("col", None, None)),
-        out_specs=(data, P(None, "row", "col"), P("col", None, None)),
+        in_specs=(data, data, P(COL, None, None)),
+        out_specs=(data, P(None, "row", COL), P(COL, None, None)),
         check_vma=False,
     )

time: 204 us -> 200 us (0.980)
  waiting for transfers between devices: 57.2 us -> 53.4 us
  starting transfers between devices: 34.6 us -> 37.7 us
    ppermute x1, starting transfers between devices: 7.33 us -> 12.6 us  [shards(): got = lax.ppermute(sent, 'core', [(0, 1), (1, 0)])]
    ppermute x13 -> x10, waiting for transfers between devices: 36 us -> 32.2 us  [the longest x4 28.8 us: gather_rows(): below = lax.ppermute(below, COL, up)]
    ppermute x13 -> x10, starting transfers between devices: 14.4 us -> 12.3 us  [the longest x3 9.45 us: gather_rows(): above = lax.ppermute(above, COL, down)]
    all_to_all x2 -> x3, blocking collectives: 40.2 us -> 38.6 us  [spread(): lax.all_to_all(jnp.broadcast_to(share[None], (size,) + share.shape), axes...]
  transfers between devices with their start and end apart: 21 -> 18, of which waited for: 12 -> 11; matrix products, arithmetic and copies ran while one was open for 2% -> 2% of each run, Pallas kernels for 6% -> 6%
where the time goes in v1:
time: 200 us
  waiting for transfers between devices  53.4 us (27%)
  blocking collectives  48.8 us (24%)
  starting transfers between devices  37.7 us (19%)
  Pallas kernels  27.8 us (14%)
  between operations  14.4 us (7%)
  matrix products  9.41 us (5%)
  other arithmetic  4.16 us (2%)
  local copies, waits for them, and re-layouts  3.96 us (2%)
    all_to_all x3, blocking collectives, spread(): lax.all_to_all(jnp.broadcast_to(share[None], (size,) + share.shape), axes...  38.6 us
    ppermute x4, waiting for transfers between devices, gather_rows(): below = lax.ppermute(below, COL, up)  28.8 us
    ppermute x1, starting transfers between devices, shards(): got = lax.ppermute(sent, 'core', [(0, 1), (1, 0)])  12.6 us
    pallas_call x1, Pallas kernels, last_factor(): pl.pallas_call(last_factor_kernel, in_specs=[pl.BlockSpec(memory_space=pl...  11.3 us
    pallas_call x1, Pallas kernels, next_factor(): pl.pallas_call(next_factor_kernel, out_shape=jax.ShapeDtypeStruct((KV, RA...  10.9 us
    all_to_all x1, blocking collectives, sum_over_rows(): lax.all_to_all(partial.reshape(NX * NY, -1, RANK), ('x', 'row'), 0, 0)  10.2 us
    ppermute x3, waiting for transfers between devices, gather_rows(): came = [lax.ppermute(piece(d), 'x', ring(NX, d)) for d in (2, 1, 3)]  10.1 us
    ppermute x3, starting transfers between devices, gather_rows(): above = lax.ppermute(above, COL, down)  9.45 us
  transfers between devices with their start and end apart: 18, of which 11 were waited for; matrix products, arithmetic and copies ran while one was open for 2% of the time, Pallas kernels for 6%

profile of v1, /device:TPU:1, one launch (start us, length us, event | category | flops | bytes accessed | tf_op | source)
XLA Modules:
  0.0 199.7 jit_solution(17831113033283303286)
XLA Ops:
  7.2 0.0 copy-start
  7.2 0.0 copy-start.3
  7.2 0.0 all-gather.5.cloned.1.call-start
  7.2 1.6 add_bitcast_fusion
  8.8 3.3 %collective-permute-start = (f32[2048,128]{1,0:T(8,128)S(1)}, f32[2048,128]{1,0:T(8,128)}, u32[]{:S(2)}, u32[]{:S(2)}) collective-permute-start(f32[2048,128]{1,0:T(8,128)S(1)} %add_bitcast_fusion), channel_id=1, source_target_pairs={{0,32},{32,0},{1,33},{33,1},{2,34},{34,2},{3,35},{35,3},{4,36},{36... | collective-permute-start | bytes 3145736 | tf_op jit(solution)/shard_map/ppermute | solution.py:252
  12.2 2.4 %collective-permute-done = f32[2048,128]{1,0:T(8,128)} collective-permute-done((f32[2048,128]{1,0:T(8,128)S(1)}, f32[2048,128]{1,0:T(8,128)}, u32[]{:S(2)}, u32[]{:S(2)}) %collective-permute-start) | collective-permute-done | bytes 1048608 | tf_op jit(solution)/shard_map/ppermute | solution.py:252
  14.6 1.5 bitcast_add_fusion
  16.1 0.1 dynamic-slice_bitcast_fusion.2
  16.2 0.1 collective-permute-start.1
  16.2 1.9 collective-permute-start.3
  18.2 1.2 collective-permute-start.2
  19.3 0.1 constant_dynamic-slice_fusion
  19.4 0.7 copy.12
  20.1 0.0 all-gather.5.cloned.1.call-update
  20.1 5.6 %collective-permute-done.1 = f32[512,128]{1,0:T(8,128)S(1)} collective-permute-done((f32[512,128]{1,0:T(8,128)S(1)}, f32[512,128]{1,0:T(8,128)S(1)}, u32[]{:S(2)}, u32[]{:S(2)}) %collective-permute-start.1) | collective-permute-done | bytes 262176 | tf_op jit(solution)/shard_map/ppermute | solution.py:255
  25.7 4.2 %collective-permute-done.3 = f32[512,128]{1,0:T(8,128)S(1)} collective-permute-done((f32[512,128]{1,0:T(8,128)S(1)}, f32[512,128]{1,0:T(8,128)S(1)}, u32[]{:S(2)}, u32[]{:S(2)}) %collective-permute-start.3) | collective-permute-done | bytes 262176 | tf_op jit(solution)/shard_map/ppermute | solution.py:255
  29.9 0.7 copy-done.7
  30.6 0.4 collective-permute-done.2
  31.0 0.2 broadcast_in_dim.44
  31.2 0.7 copy-done.6
  31.9 0.1 copy-done.8
  32.0 1.0 constant_dynamic-update-slice_fusion.7
  33.0 1.3 collective-permute-start.4
  34.3 4.0 %collective-permute-start.5 = (f32[512,128]{1,0:T(8,128)S(1)}, f32[512,128]{1,0:T(8,128)S(1)}, u32[]{:S(2)}, u32[]{:S(2)}) collective-permute-start(f32[512,128]{1,0:T(8,128)S(1)} %get-tuple-element.4), channel_id=1, source_target_pairs={{0,7},{1,0},{2,1},{3,2},{4,3},{5,4},{6,5},{7,6},{8,15},{9,8},{10,9... | collective-permute-start | bytes 786440 | tf_op jit(solution)/shard_map/ppermute | solution.py:265
  38.3 9.5 %collective-permute-done.4 = f32[512,128]{1,0:T(8,128)S(1)} collective-permute-done((f32[512,128]{1,0:T(8,128)S(1)}, f32[512,128]{1,0:T(8,128)S(1)}, u32[]{:S(2)}, u32[]{:S(2)}) %collective-permute-start.4) | collective-permute-done | bytes 262176 | tf_op jit(solution)/shard_map/ppermute | solution.py:262
  47.8 0.0 collective-permute-start.6
  47.8 0.0 collective-permute-done.5
  47.8 2.7 %collective-permute-start.7 = (f32[512,128]{1,0:T(8,128)S(1)}, f32[512,128]{1,0:T(8,128)S(1)}, u32[]{:S(2)}, u32[]{:S(2)}) collective-permute-start(f32[512,128]{1,0:T(8,128)S(1)} %collective-permute-done.5), channel_id=1, source_target_pairs={{0,7},{1,0},{2,1},{3,2},{4,3},{5,4},{6,5},{7,6},{8,15},{9,8},{10,9... | collective-permute-start | bytes 786440 | tf_op jit(solution)/shard_map/ppermute | solution.py:265
  50.5 8.5 %collective-permute-done.6 = f32[512,128]{1,0:T(8,128)S(1)} collective-permute-done((f32[512,128]{1,0:T(8,128)S(1)}, f32[512,128]{1,0:T(8,128)S(1)}, u32[]{:S(2)}, u32[]{:S(2)}) %collective-permute-start.6) | collective-permute-done | bytes 262176 | tf_op jit(solution)/shard_map/ppermute | solution.py:262
  58.9 0.0 collective-permute-start.8
  59.0 0.0 collective-permute-done.7
  59.0 2.7 %collective-permute-start.9 = (f32[512,128]{1,0:T(8,128)S(1)}, f32[512,128]{1,0:T(8,128)S(1)}, u32[]{:S(2)}, u32[]{:S(2)}) collective-permute-start(f32[512,128]{1,0:T(8,128)S(1)} %collective-permute-done.7), channel_id=1, source_target_pairs={{0,7},{1,0},{2,1},{3,2},{4,3},{5,4},{6,5},{7,6},{8,15},{9,8},{10,9... | collective-permute-start | bytes 786440 | tf_op jit(solution)/shard_map/ppermute | solution.py:265
  61.8 4.5 %collective-permute-done.8 = f32[512,128]{1,0:T(8,128)S(1)} collective-permute-done((f32[512,128]{1,0:T(8,128)S(1)}, f32[512,128]{1,0:T(8,128)S(1)}, u32[]{:S(2)}, u32[]{:S(2)}) %collective-permute-start.8) | collective-permute-done | bytes 262176 | tf_op jit(solution)/shard_map/ppermute | solution.py:262
  66.3 0.0 collective-permute-start.10
  66.4 0.0 collective-permute-done.9
  66.4 6.3 %collective-permute-done.10 = f32[512,128]{1,0:T(8,128)S(1)} collective-permute-done((f32[512,128]{1,0:T(8,128)S(1)}, f32[512,128]{1,0:T(8,128)S(1)}, u32[]{:S(2)}, u32[]{:S(2)}) %collective-permute-start.10) | collective-permute-done | bytes 262176 | tf_op jit(solution)/shard_map/ppermute | solution.py:262
  72.8 0.0 all-gather.5.cloned.1.call-done
  72.8 3.0 %fusion.9 = f32[512,256]{1,0:T(8,128)S(1)} fusion(f32[512,1024]{1,0:T(8,128)S(1)} %constant_dynamic-update-slice_fusion, f32[1024,1,256]{2,0,1:T(8,128)} %all-gather.5.cloned.1.call-done), kind=kOutput, calls=%fused_computation.28 | convolution fusion | flops 1610612736 | bytes 3670016 | tf_op jit(solution)/shard_map/dot_general | solution.py:27
  75.9 1.7 fusion.2
  77.6 6.3 %all-to-all-start = ((f32[16,16,256]{2,1,0:T(8,128)}), f32[16,16,256]{2,1,0:T(8,128)S(1)}, u32[]{:S(2)}, u32[]{:S(2)}) async-start(f32[16,16,256]{2,1,0:T(8,128)} %bitcast.9), calls=%async_computation | async-start | bytes 524288 | tf_op jit(solution)/shard_map/all_to_all | solution.py:236
  83.9 0.0 all-gather.7.cloned.1.call-start
  84.0 7.2 %all-to-all-done = f32[16,16,256]{2,1,0:T(8,128)S(1)} async-done(((f32[16,16,256]{2,1,0:T(8,128)}), f32[16,16,256]{2,1,0:T(8,128)S(1)}, u32[]{:S(2)}, u32[]{:S(2)}) %all-to-all-start) | async-done | bytes 262176 | tf_op jit(solution)/shard_map/all_to_all | solution.py:236
  91.3 0.6 collective-permute-start.13
  91.9 0.9 collective-permute-start.11
  92.8 3.5 %collective-permute-done.11 = f32[16,256]{1,0:T(8,128)S(1)} collective-permute-done((f32[16,256]{1,0:T(8,128)S(1)}, f32[16,256]{1,0:T(8,128)S(1)}, u32[]{:S(2)}, u32[]{:S(2)}) %collective-permute-start.11) | collective-permute-done | bytes 16416 | tf_op jit(solution)/shard_map/ppermute | solution.py:221
  96.3 0.0 collective-permute-done.12
  96.3 0.0 collective-permute-done.13
  96.3 0.1 broadcast_in_dim.50
  96.5 15.2 %all_to_all.25 = f32[16,4,16,256]{3,2,1,0:T(8,128)S(1)} all-to-all(f32[16,4,16,256]{3,2,1,0:T(8,128)S(1)} %broadcast_in_dim.50), channel_id=1, replica_groups=mesh['x'=4,'core'=2,'row'=4,'quad'=2,'place'=4] {'x','row'}, dimensions={0} | all-to-all | bytes 2097152 | tf_op jit(solution)/shard_map/all_to_all | solution.py:228
  111.6 0.1 copy.10
  111.7 10.9 %next_factor.1.factor_ref = f32[1024,256]{1,0:T(8,128)S(1)} custom-call(f32[1024,256]{1,0:T(8,128)S(1)} %bitcast.48, f32[1024,256]{1,0:T(8,128)S(1)} %bitcast.47), custom_call_target="tpu_custom_call" | custom-call | tf_op jit(solution)/shard_map/next_factor/pallas_call | solution.py:127
  122.7 2.6 %fusion.12 = f32[512,256]{1,0:T(8,128)} fusion(f32[512,1024]{1,0:T(8,128)S(1)} %constant_dynamic-update-slice_fusion, f32[1024,256]{1,0:T(8,128)S(1)} %next_factor.1.factor_ref), kind=kOutput, calls=%fused_computation.30 | convolution fusion | flops 1610612736 | bytes 3670016 | tf_op jit(solution)/shard_map/dot_general | solution.py:27
  125.3 0.0 all-gather.7.cloned.1.call-update
  125.3 2.1 %fusion = f32[256,256]{1,0:T(8,128)S(1)} fusion(f32[512,256]{1,0:T(8,128)} %fusion.12, f32[512,1024]{1,0:T(8,128)S(1)} %constant_dynamic-update-slice_fusion, s32[]{:T(128)S(6)} %select_n.80), kind=kOutput, calls=%fused_computation.2 | convolution fusion | flops 402653184 | bytes 1310724 | tf_op jit(solution)/shard_map/dot_general | solution.py:27
  127.4 10.2 %all_to_all.26 = f32[16,16,256]{2,1,0:T(8,128)S(1)} all-to-all(f32[16,16,256]{2,1,0:T(8,128)S(1)} %bitcast.55), channel_id=1, replica_groups=mesh['x'=4,'core'=2,'row'=4,'quad'=2,'place'=4] {'x','row'}, dimensions={0} | all-to-all | bytes 524288 | tf_op jit(solution)/shard_map/all_to_all | solution.py:236
  137.6 11.2 %all_to_all.27 = f32[16,16,256]{2,1,0:T(8,128)S(1)} all-to-all(f32[16,16,256]{2,1,0:T(8,128)S(1)} %broadcast_in_dim.52), channel_id=1, replica_groups=mesh['x'=4,'core'=2,'row'=4,'quad'=2,'place'=4] {'x','place'}, dimensions={0} | all-to-all | bytes 524288 | tf_op jit(solution)/shard_map/all_to_all | solution.py:228
  148.8 0.1 broadcast_in_dim.53
  148.9 12.2 %all_to_all.28 = f32[4,16,16,256]{3,2,1,0:T(8,128)S(1)} all-to-all(f32[4,16,16,256]{3,2,1,0:T(8,128)S(1)} %broadcast_in_dim.53), channel_id=1, replica_groups=mesh['x'=4,'core'=2,'row'=4,'quad'=2,'place'=4] {'row'}, dimensions={0} | all-to-all | bytes 2097152 | tf_op jit(solution)/shard_map/all_to_all | solution.py:228
  161.1 0.1 copy.11
  161.2 11.3 %last_factor.1.own_ref = f32[384,256]{1,0:T(8,128)S(1)} custom-call(s32[1]{0:T(128)} %bitcast.17.col_ref, f32[1024,256]{1,0:T(8,128)S(1)} %bitcast.49, f32[1024,256]{1,0:T(8,128)S(1)} %next_factor.1.factor_ref), custom_call_target="tpu_custom_call" | custom-call | tf_op jit(solution)/shard_map/last_factor/pallas_call | solution.py:138
  172.5 12.6 %collective-permute-start.14 = (f32[384,256]{1,0:T(8,128)S(1)}, f32[384,256]{1,0:T(8,128)S(1)}, u32[]{:S(2)}, u32[]{:S(2)}) collective-permute-start(f32[384,256]{1,0:T(8,128)S(1)} %last_factor.1.own_ref), channel_id=1, source_target_pairs={{0,32},{32,0},{1,33},{33,1},{2,34},{34,2},{3,35},{35,3},{4,36},{36... | collective-permute-start | bytes 1179656 | tf_op jit(solution)/shard_map/ppermute | solution.py:287
  185.1 1.3 collective-permute-done.14.got_ref
  186.5 0.7 copy-done.4
  187.2 5.6 %outputs.1 = (f32[1,2,2048,128]{3,2,1,0:T(8,128)}, bf16[2,2048,128]{2,1,0:T(8,128)(2,1)}, f32[128,2,256]{2,1,0:T(2,128)}) custom-call(s32[1]{0:T(128)} %bitcast.core_ref, f32[4,2,512,256]{3,2,1,0:T(8,128)} %bitcast.50, f32[384,256]{1,0:T(8,128)} %copy-done.2, f32[384,256]{1,0:T(8,128)} %copy-done.4, f32[1,2,2048,128]{3,2,1,0:T(8,128)} %momentum_ref.1, ...), custom_call_target="tpu_custom_call" | custom-call | tf_op jit(solution)/shard_map/outputs/pallas_call | solution.py:185
  (29 shorter events, 0.3 us)
Async XLA Ops:
  7.2 12.2 %copy-start = (f32[128,2,256]{2,1,0:T(2,128)S(1)}, f32[128,2,256]{2,1,0:T(2,128)}, u32[]{:S(2)}) copy-start(f32[128,2,256]{2,1,0:T(2,128)} %param.5) | copy-start | bytes 786436
  7.2 7.4 %copy-start.3 = (f32[1,2,2048,128]{3,2,1,0:T(8,128)S(1)}, f32[1,2,2048,128]{3,2,1,0:T(8,128)}, u32[]{:S(2)}) copy-start(f32[1,2,2048,128]{3,2,1,0:T(8,128)} %momentum_ref.1) | copy-start | bytes 6291460
  7.2 65.6 %all-gather.5.cloned.1.call-start = ((), (), s32[]{:S(2)}) async-start(), calls=%async_computation.5 | async-start | bytes 1179648 | tf_op jit(solution)/shard_map/all_gather | solution.py:276
  8.8 5.7 %collective-permute-start = (f32[2048,128]{1,0:T(8,128)S(1)}, f32[2048,128]{1,0:T(8,128)}, u32[]{:S(2)}, u32[]{:S(2)}) collective-permute-start(f32[2048,128]{1,0:T(8,128)S(1)} %add_bitcast_fusion), channel_id=1, source_target_pairs={{0,32},{32,0},{1,33},{33,1},{2,34},{34,2},{3,35},{35,3},{4,36},{36... | collective-permute-start | bytes 3145736 | tf_op jit(solution)/shard_map/ppermute | solution.py:252
  16.2 9.5 %collective-permute-start.1 = (f32[512,128]{1,0:T(8,128)S(1)}, f32[512,128]{1,0:T(8,128)S(1)}, u32[]{:S(2)}, u32[]{:S(2)}) collective-permute-start(f32[512,128]{1,0:T(8,128)S(1)} %get-tuple-element.5), channel_id=1, source_target_pairs={{0,64},{64,128},{128,192},{192,0},{1,65},{65,129},{129,193},{193,1... | collective-permute-start | bytes 786440 | tf_op jit(solution)/shard_map/ppermute | solution.py:255
  16.2 13.6 %collective-permute-start.3 = (f32[512,128]{1,0:T(8,128)S(1)}, f32[512,128]{1,0:T(8,128)S(1)}, u32[]{:S(2)}, u32[]{:S(2)}) collective-permute-start(f32[512,128]{1,0:T(8,128)S(1)} %get-tuple-element.6), channel_id=1, source_target_pairs={{0,128},{64,192},{128,0},{192,64},{1,129},{65,193},{129,1},{193,65... | collective-permute-start | bytes 786440 | tf_op jit(solution)/shard_map/ppermute | solution.py:255
  18.2 12.8 %collective-permute-start.2 = (f32[512,128]{1,0:T(8,128)S(1)}, f32[512,128]{1,0:T(8,128)}, u32[]{:S(2)}, u32[]{:S(2)}) collective-permute-start(f32[512,128]{1,0:T(8,128)S(1)} %get-tuple-element.7), channel_id=1, source_target_pairs={{0,192},{64,0},{128,64},{192,128},{1,193},{65,1},{129,65},{193,129... | collective-permute-start | bytes 786440 | tf_op jit(solution)/shard_map/ppermute | solution.py:255
  25.7 4.2 %copy-start.5 = (f32[512,128]{1,0:T(8,128)}, f32[512,128]{1,0:T(8,128)S(1)}, u32[]{:S(2)}) copy-start(f32[512,128]{1,0:T(8,128)S(1)} %collective-permute-done.1) | copy-start | bytes 786436
  29.9 0.7 copy-start.7
  31.0 1.0 copy-start.6
  31.0 1.0 copy-start.8
  33.0 14.7 %collective-permute-start.4 = (f32[512,128]{1,0:T(8,128)S(1)}, f32[512,128]{1,0:T(8,128)S(1)}, u32[]{:S(2)}, u32[]{:S(2)}) collective-permute-start(f32[512,128]{1,0:T(8,128)S(1)} %get-tuple-element.4), channel_id=1, source_target_pairs={{0,1},{1,2},{2,3},{3,4},{4,5},{5,6},{6,7},{7,0},{8,9},{9,10},{10,1... | collective-permute-start | bytes 786440 | tf_op jit(solution)/shard_map/ppermute | solution.py:262
  34.3 13.5 %collective-permute-start.5 = (f32[512,128]{1,0:T(8,128)S(1)}, f32[512,128]{1,0:T(8,128)S(1)}, u32[]{:S(2)}, u32[]{:S(2)}) collective-permute-start(f32[512,128]{1,0:T(8,128)S(1)} %get-tuple-element.4), channel_id=1, source_target_pairs={{0,7},{1,0},{2,1},{3,2},{4,3},{5,4},{6,5},{7,6},{8,15},{9,8},{10,9... | collective-permute-start | bytes 786440 | tf_op jit(solution)/shard_map/ppermute | solution.py:265
  47.8 11.2 %collective-permute-start.6 = (f32[512,128]{1,0:T(8,128)S(1)}, f32[512,128]{1,0:T(8,128)S(1)}, u32[]{:S(2)}, u32[]{:S(2)}) collective-permute-start(f32[512,128]{1,0:T(8,128)S(1)} %collective-permute-done.4), channel_id=1, source_target_pairs={{0,1},{1,2},{2,3},{3,4},{4,5},{5,6},{6,7},{7,0},{8,9},{9,10},{10,1... | collective-permute-start | bytes 786440 | tf_op jit(solution)/shard_map/ppermute | solution.py:262
  47.8 11.2 %collective-permute-start.7 = (f32[512,128]{1,0:T(8,128)S(1)}, f32[512,128]{1,0:T(8,128)S(1)}, u32[]{:S(2)}, u32[]{:S(2)}) collective-permute-start(f32[512,128]{1,0:T(8,128)S(1)} %collective-permute-done.5), channel_id=1, source_target_pairs={{0,7},{1,0},{2,1},{3,2},{4,3},{5,4},{6,5},{7,6},{8,15},{9,8},{10,9... | collective-permute-start | bytes 786440 | tf_op jit(solution)/shard_map/ppermute | solution.py:265
  58.9 7.4 %collective-permute-start.8 = (f32[512,128]{1,0:T(8,128)S(1)}, f32[512,128]{1,0:T(8,128)S(1)}, u32[]{:S(2)}, u32[]{:S(2)}) collective-permute-start(f32[512,128]{1,0:T(8,128)S(1)} %collective-permute-done.6), channel_id=1, source_target_pairs={{0,1},{1,2},{2,3},{3,4},{4,5},{5,6},{6,7},{7,0},{8,9},{9,10},{10,1... | collective-permute-start | bytes 786440 | tf_op jit(solution)/shard_map/ppermute | solution.py:262
  59.0 7.4 %collective-permute-start.9 = (f32[512,128]{1,0:T(8,128)S(1)}, f32[512,128]{1,0:T(8,128)S(1)}, u32[]{:S(2)}, u32[]{:S(2)}) collective-permute-start(f32[512,128]{1,0:T(8,128)S(1)} %collective-permute-done.7), channel_id=1, source_target_pairs={{0,7},{1,0},{2,1},{3,2},{4,3},{5,4},{6,5},{7,6},{8,15},{9,8},{10,9... | collective-permute-start | bytes 786440 | tf_op jit(solution)/shard_map/ppermute | solution.py:265
  66.3 6.4 %collective-permute-start.10 = (f32[512,128]{1,0:T(8,128)S(1)}, f32[512,128]{1,0:T(8,128)S(1)}, u32[]{:S(2)}, u32[]{:S(2)}) collective-permute-start(f32[512,128]{1,0:T(8,128)S(1)} %collective-permute-done.8), channel_id=1, source_target_pairs={{0,1},{1,2},{2,3},{3,4},{4,5},{5,6},{6,7},{7,0},{8,9},{9,10},{10,1... | collective-permute-start | bytes 786440 | tf_op jit(solution)/shard_map/ppermute | solution.py:262
  77.6 13.6 %all-to-all-start = ((f32[16,16,256]{2,1,0:T(8,128)}), f32[16,16,256]{2,1,0:T(8,128)S(1)}, u32[]{:S(2)}, u32[]{:S(2)}) async-start(f32[16,16,256]{2,1,0:T(8,128)} %bitcast.9), calls=%async_computation | async-start | bytes 524288 | tf_op jit(solution)/shard_map/all_to_all | solution.py:236
  83.9 102.6 %all-gather.7.cloned.1.call-start = ((), (), s32[]{:S(2)}) async-start(), calls=%async_computation.6 | async-start | bytes 4718592 | tf_op jit(solution)/shard_map/all_gather | solution.py:284
  91.3 5.0 %collective-permute-start.13 = (f32[16,256]{1,0:T(8,128)S(1)}, f32[16,256]{1,0:T(8,128)S(1)}, u32[]{:S(2)}, u32[]{:S(2)}) collective-permute-start(f32[16,256]{1,0:T(8,128)S(1)} %reduce_sum.18), channel_id=1, source_target_pairs={{0,3},{1,0},{2,1},{3,2},{4,7},{5,4},{6,5},{7,6},{8,11},{9,8},{10,9... | collective-permute-start | bytes 49160 | tf_op jit(solution)/shard_map/ppermute | solution.py:221
  91.9 4.4 %collective-permute-start.12 = (f32[16,256]{1,0:T(8,128)S(1)}, f32[16,256]{1,0:T(8,128)S(1)}, u32[]{:S(2)}, u32[]{:S(2)}) collective-permute-start(f32[16,256]{1,0:T(8,128)S(1)} %reduce_sum.18), channel_id=1, source_target_pairs={{0,2},{1,3},{2,0},{3,1},{4,6},{5,7},{6,4},{7,5},{8,10},{9,11},{10,... | collective-permute-start | bytes 49160 | tf_op jit(solution)/shard_map/ppermute | solution.py:221
  91.9 4.4 %collective-permute-start.11 = (f32[16,256]{1,0:T(8,128)S(1)}, f32[16,256]{1,0:T(8,128)S(1)}, u32[]{:S(2)}, u32[]{:S(2)}) collective-permute-start(f32[16,256]{1,0:T(8,128)S(1)} %reduce_sum.18), channel_id=1, source_target_pairs={{0,1},{1,2},{2,3},{3,0},{4,5},{5,6},{6,7},{7,4},{8,9},{9,10},{10,1... | collective-permute-start | bytes 49160 | tf_op jit(solution)/shard_map/ppermute | solution.py:221
  96.4 15.3 %copy-start.1 = (f32[1024,1,256]{2,0,1:T(8,128)S(1)}, f32[1024,1,256]{2,0,1:T(8,128)}, u32[]{:S(2)}) copy-start(f32[1024,1,256]{2,0,1:T(8,128)} %all-gather.5.cloned.1.call-done) | copy-start | bytes 3145732
  172.5 13.9 %copy-start.2 = (f32[384,256]{1,0:T(8,128)}, f32[384,256]{1,0:T(8,128)S(1)}, u32[]{:S(2)}) copy-start(f32[384,256]{1,0:T(8,128)S(1)} %last_factor.1.own_ref) | copy-start | bytes 1179652
  172.5 13.9 %collective-permute-start.14 = (f32[384,256]{1,0:T(8,128)S(1)}, f32[384,256]{1,0:T(8,128)S(1)}, u32[]{:S(2)}, u32[]{:S(2)}) collective-permute-start(f32[384,256]{1,0:T(8,128)S(1)} %last_factor.1.own_ref), channel_id=1, source_target_pairs={{0,32},{32,0},{1,33},{33,1},{2,34},{34,2},{3,35},{35,3},{4,36},{36... | collective-permute-start | bytes 1179656 | tf_op jit(solution)/shard_map/ppermute | solution.py:287
  186.5 0.7 copy-start.4
Sparse Core Ops, SparseCore 0:
  20.2 37.1 all-gather.4
  125.4 40.7 all-gather.6

commit v2 on v1

--- a/solution.py
+++ b/solution.py
@@ -257,13 +257,15 @@
 
     up, down = ring(NZ, 1), ring(NZ, -1)
     below = above = block
-    parts = [(0, block)]
+    parts = []
     for step in range(1, NZ // 2 + 1):
         below = lax.ppermute(below, COL, up)
         parts.append((NZ - step, below))
         if step < NZ // 2:
             above = lax.ppermute(above, COL, down)
             parts.append((step, above))
+        if step == 1:
+            parts.append((0, block))
     rows = jnp.zeros((block.shape[0], KV), jnp.float32)
     for offset, part in parts:
         rows = lax.dynamic_update_slice(rows, part, (0, lax.rem(z + offset, NZ) * WIDTH))
@@ -273,6 +275,7 @@
 def shards(grad, momentum, right_factor):
     core = lax.axis_index("core")
     own_factor = lax.dynamic_index_in_dim(right_factor, core, 1, False)
+    own_factor, momentum, grad = lax.optimization_barrier((own_factor, momentum, grad))
     factor = lax.all_gather(own_factor, COL, axis=0, tiled=True)
     rows = gather_rows(grad, momentum)
 

time: 200 us -> 199 us (level)
  starting transfers between devices: 37.7 us -> 39.7 us
    ppermute x4, waiting for transfers between devices: 28.8 us -> 26.1 us  [gather_rows(): below = lax.ppermute(below, COL, up)]
  transfers between devices with their start and end apart: 18 -> 18, of which waited for: 11 -> 12; matrix products, arithmetic and copies ran while one was open for 2% -> 1% of each run, Pallas kernels for 6% -> 6%
where the time goes in v2:
time: 199 us
  waiting for transfers between devices  52.5 us (26%)
  blocking collectives  48.7 us (24%)
  starting transfers between devices  39.7 us (20%)
  Pallas kernels  27.8 us (14%)
  between operations  14.4 us (7%)
  matrix products  9.41 us (5%)
  local copies, waits for them, and re-layouts  3.38 us (2%)
  other arithmetic  3.03 us (2%)
    all_to_all x3, blocking collectives, spread(): lax.all_to_all(jnp.broadcast_to(share[None], (size,) + share.shape), axes...  38.2 us
    ppermute x4, waiting for transfers between devices, gather_rows(): below = lax.ppermute(below, COL, up)  26.1 us
    ppermute x1, starting transfers between devices, shards(): got = lax.ppermute(sent, 'core', [(0, 1), (1, 0)])  11.6 us
    ppermute x3, waiting for transfers between devices, gather_rows(): came = [lax.ppermute(piece(d), 'x', ring(NX, d)) for d in (2, 1, 3)]  11.5 us
    pallas_call x1, Pallas kernels, last_factor(): pl.pallas_call(last_factor_kernel, in_specs=[pl.BlockSpec(memory_space=pl...  11.3 us
    pallas_call x1, Pallas kernels, next_factor(): pl.pallas_call(next_factor_kernel, out_shape=jax.ShapeDtypeStruct((KV, RA...  10.9 us
    all_to_all x1, blocking collectives, sum_over_rows(): lax.all_to_all(partial.reshape(NX * NY, -1, RANK), ('x', 'row'), 0, 0)  10.6 us
    ppermute x3, starting transfers between devices, gather_rows(): above = lax.ppermute(above, COL, down)  10.2 us
  transfers between devices with their start and end apart: 18, of which 12 were waited for; matrix products, arithmetic and copies ran while one was open for 1% of the time, Pallas kernels for 6%

profile of v2, /device:TPU:1, one launch (start us, length us, event | category | flops | bytes accessed | tf_op | source)
XLA Modules:
  0.0 199.0 jit_solution(6927511295741531243)
XLA Ops:
  7.2 0.0 copy-start
  7.2 0.0 copy-start.3
  7.2 0.0 all-gather.4.cloned.1.call-start
  7.2 0.9 copy-done
  8.1 0.1 constant_dynamic-slice_fusion
  8.2 0.7 copy.13
  8.9 1.4 add_bitcast_fusion
  10.4 3.3 %collective-permute-start = (f32[2048,128]{1,0:T(8,128)S(1)}, f32[2048,128]{1,0:T(8,128)}, u32[]{:S(2)}, u32[]{:S(2)}) collective-permute-start(f32[2048,128]{1,0:T(8,128)S(1)} %add_bitcast_fusion), channel_id=1, source_target_pairs={{0,32},{32,0},{1,33},{33,1},{2,34},{34,2},{3,35},{35,3},{4,36},{36... | collective-permute-start | bytes 3145736 | tf_op jit(solution)/shard_map/ppermute | solution.py:252
  13.7 2.4 %collective-permute-done = f32[2048,128]{1,0:T(8,128)} collective-permute-done((f32[2048,128]{1,0:T(8,128)S(1)}, f32[2048,128]{1,0:T(8,128)}, u32[]{:S(2)}, u32[]{:S(2)}) %collective-permute-start) | collective-permute-done | bytes 1048608 | tf_op jit(solution)/shard_map/ppermute | solution.py:252
  16.1 1.5 bitcast_add_fusion
  17.6 0.1 dynamic-slice_bitcast_fusion.2
  17.7 0.1 collective-permute-start.1
  17.8 1.9 collective-permute-start.3
  19.7 1.2 collective-permute-start.2
  20.8 0.0 all-gather.4.cloned.1.call-update
  20.9 6.4 %collective-permute-done.1 = f32[512,128]{1,0:T(8,128)S(1)} collective-permute-done((f32[512,128]{1,0:T(8,128)S(1)}, f32[512,128]{1,0:T(8,128)S(1)}, u32[]{:S(2)}, u32[]{:S(2)}) %collective-permute-start.1) | collective-permute-done | bytes 262176 | tf_op jit(solution)/shard_map/ppermute | solution.py:255
  27.2 4.2 %collective-permute-done.3 = f32[512,128]{1,0:T(8,128)S(1)} collective-permute-done((f32[512,128]{1,0:T(8,128)S(1)}, f32[512,128]{1,0:T(8,128)S(1)}, u32[]{:S(2)}, u32[]{:S(2)}) %collective-permute-start.3) | collective-permute-done | bytes 262176 | tf_op jit(solution)/shard_map/ppermute | solution.py:255
  31.4 1.0 collective-permute-done.2
  32.4 0.1 fusion.6
  32.4 0.0 copy-start.4
  32.5 0.7 collective-permute-start.4
  33.1 4.0 %collective-permute-start.5 = (f32[512,128]{1,0:T(8,128)S(1)}, f32[512,128]{1,0:T(8,128)S(1)}, u32[]{:S(2)}, u32[]{:S(2)}) collective-permute-start(f32[512,128]{1,0:T(8,128)S(1)} %fusion.6), channel_id=1, source_target_pairs={{0,7},{1,0},{2,1},{3,2},{4,3},{5,4},{6,5},{7,6},{8,15},{9,8},{10,9... | collective-permute-start | bytes 786440 | tf_op jit(solution)/shard_map/ppermute | solution.py:265
  37.1 8.0 %collective-permute-done.4 = f32[512,128]{1,0:T(8,128)S(1)} collective-permute-done((f32[512,128]{1,0:T(8,128)S(1)}, f32[512,128]{1,0:T(8,128)S(1)}, u32[]{:S(2)}, u32[]{:S(2)}) %collective-permute-start.4) | collective-permute-done | bytes 262176 | tf_op jit(solution)/shard_map/ppermute | solution.py:262
  45.1 0.0 collective-permute-start.6
  45.1 0.1 collective-permute-done.5
  45.2 3.5 %collective-permute-start.7 = (f32[512,128]{1,0:T(8,128)S(1)}, f32[512,128]{1,0:T(8,128)S(1)}, u32[]{:S(2)}, u32[]{:S(2)}) collective-permute-start(f32[512,128]{1,0:T(8,128)S(1)} %collective-permute-done.5), channel_id=1, source_target_pairs={{0,7},{1,0},{2,1},{3,2},{4,3},{5,4},{6,5},{7,6},{8,15},{9,8},{10,9... | collective-permute-start | bytes 786440 | tf_op jit(solution)/shard_map/ppermute | solution.py:265
  48.7 0.2 broadcast_in_dim.44
  49.0 7.5 %collective-permute-done.6 = f32[512,128]{1,0:T(8,128)S(1)} collective-permute-done((f32[512,128]{1,0:T(8,128)S(1)}, f32[512,128]{1,0:T(8,128)S(1)}, u32[]{:S(2)}, u32[]{:S(2)}) %collective-permute-start.6) | collective-permute-done | bytes 262176 | tf_op jit(solution)/shard_map/ppermute | solution.py:262
  56.5 0.0 collective-permute-start.8
  56.6 0.0 collective-permute-done.7
  56.6 2.7 %collective-permute-start.9 = (f32[512,128]{1,0:T(8,128)S(1)}, f32[512,128]{1,0:T(8,128)S(1)}, u32[]{:S(2)}, u32[]{:S(2)}) collective-permute-start(f32[512,128]{1,0:T(8,128)S(1)} %collective-permute-done.7), channel_id=1, source_target_pairs={{0,7},{1,0},{2,1},{3,2},{4,3},{5,4},{6,5},{7,6},{8,15},{9,8},{10,9... | collective-permute-start | bytes 786440 | tf_op jit(solution)/shard_map/ppermute | solution.py:265
  59.4 4.2 %collective-permute-done.8 = f32[512,128]{1,0:T(8,128)S(1)} collective-permute-done((f32[512,128]{1,0:T(8,128)S(1)}, f32[512,128]{1,0:T(8,128)S(1)}, u32[]{:S(2)}, u32[]{:S(2)}) %collective-permute-start.8) | collective-permute-done | bytes 262176 | tf_op jit(solution)/shard_map/ppermute | solution.py:262
  63.6 0.0 collective-permute-start.10
  63.7 0.0 collective-permute-done.9
  63.7 6.3 %collective-permute-done.10 = f32[512,128]{1,0:T(8,128)S(1)} collective-permute-done((f32[512,128]{1,0:T(8,128)S(1)}, f32[512,128]{1,0:T(8,128)S(1)}, u32[]{:S(2)}, u32[]{:S(2)}) %collective-permute-start.10) | collective-permute-done | bytes 262176 | tf_op jit(solution)/shard_map/ppermute | solution.py:262
  70.0 0.0 all-gather.4.cloned.1.call-done.factor_ref
  70.1 3.0 %fusion.9 = f32[512,256]{1,0:T(8,128)S(1)} fusion(f32[512,1024]{1,0:T(8,128)S(1)} %constant_dynamic-update-slice_fusion, f32[1024,256]{1,0:T(8,128)} %all-gather.4.cloned.1.call-done.factor_ref), kind=kOutput, calls=%fused_computation.29 | convolution fusion | flops 1610612736 | bytes 3670016 | tf_op jit(solution)/shard_map/dot_general | solution.py:27
  73.1 1.7 fusion.2
  74.8 8.1 %all-to-all-start = ((f32[16,16,256]{2,1,0:T(8,128)}), f32[16,16,256]{2,1,0:T(8,128)S(1)}, u32[]{:S(2)}, u32[]{:S(2)}) async-start(f32[16,16,256]{2,1,0:T(8,128)} %bitcast.9), calls=%async_computation | async-start | bytes 524288 | tf_op jit(solution)/shard_map/all_to_all | solution.py:236
  83.0 0.0 all-gather.6.cloned.1.call-start
  83.1 7.2 %all-to-all-done = f32[16,16,256]{2,1,0:T(8,128)S(1)} async-done(((f32[16,16,256]{2,1,0:T(8,128)}), f32[16,16,256]{2,1,0:T(8,128)S(1)}, u32[]{:S(2)}, u32[]{:S(2)}) %all-to-all-start) | async-done | bytes 262176 | tf_op jit(solution)/shard_map/all_to_all | solution.py:236
  90.3 1.5 collective-permute-start.13
  91.9 0.3 collective-permute-start.12
  92.2 0.5 collective-permute-start.11
  92.7 3.8 %collective-permute-done.11 = f32[16,256]{1,0:T(8,128)S(1)} collective-permute-done((f32[16,256]{1,0:T(8,128)S(1)}, f32[16,256]{1,0:T(8,128)S(1)}, u32[]{:S(2)}, u32[]{:S(2)}) %collective-permute-start.11) | collective-permute-done | bytes 16416 | tf_op jit(solution)/shard_map/ppermute | solution.py:221
  96.6 0.0 collective-permute-done.12
  96.6 0.0 collective-permute-done.13
  96.6 0.1 broadcast_in_dim.50
  96.7 15.4 %all_to_all.25 = f32[16,4,16,256]{3,2,1,0:T(8,128)S(1)} all-to-all(f32[16,4,16,256]{3,2,1,0:T(8,128)S(1)} %broadcast_in_dim.50), channel_id=1, replica_groups=mesh['x'=4,'core'=2,'row'=4,'quad'=2,'place'=4] {'x','row'}, dimensions={0} | all-to-all | bytes 2097152 | tf_op jit(solution)/shard_map/all_to_all | solution.py:228
  112.1 0.1 copy.9
  112.2 10.9 %next_factor.1.factor_ref = f32[1024,256]{1,0:T(8,128)S(1)} custom-call(f32[1024,256]{1,0:T(8,128)S(1)} %bitcast.47, f32[1024,256]{1,0:T(8,128)S(1)} %copy-done.1), custom_call_target="tpu_custom_call" | custom-call | tf_op jit(solution)/shard_map/next_factor/pallas_call | solution.py:127
  123.1 2.6 %fusion.10 = f32[512,256]{1,0:T(8,128)} fusion(f32[512,1024]{1,0:T(8,128)S(1)} %constant_dynamic-update-slice_fusion, f32[1024,256]{1,0:T(8,128)S(1)} %next_factor.1.factor_ref), kind=kOutput, calls=%fused_computation.30 | convolution fusion | flops 1610612736 | bytes 3670016 | tf_op jit(solution)/shard_map/dot_general | solution.py:27
  125.7 0.0 all-gather.6.cloned.1.call-update
  125.8 2.1 %fusion = f32[256,256]{1,0:T(8,128)S(1)} fusion(f32[512,256]{1,0:T(8,128)} %fusion.10, f32[512,1024]{1,0:T(8,128)S(1)} %constant_dynamic-update-slice_fusion, s32[]{:T(128)S(6)} %select_n.80), kind=kOutput, calls=%fused_computation.2 | convolution fusion | flops 402653184 | bytes 1310724 | tf_op jit(solution)/shard_map/dot_general | solution.py:27
  127.8 10.6 %all_to_all.26 = f32[16,16,256]{2,1,0:T(8,128)S(1)} all-to-all(f32[16,16,256]{2,1,0:T(8,128)S(1)} %bitcast.54), channel_id=1, replica_groups=mesh['x'=4,'core'=2,'row'=4,'quad'=2,'place'=4] {'x','row'}, dimensions={0} | all-to-all | bytes 524288 | tf_op jit(solution)/shard_map/all_to_all | solution.py:236
  138.4 10.6 %all_to_all.27 = f32[16,16,256]{2,1,0:T(8,128)S(1)} all-to-all(f32[16,16,256]{2,1,0:T(8,128)S(1)} %broadcast_in_dim.52), channel_id=1, replica_groups=mesh['x'=4,'core'=2,'row'=4,'quad'=2,'place'=4] {'x','place'}, dimensions={0} | all-to-all | bytes 524288 | tf_op jit(solution)/shard_map/all_to_all | solution.py:228
  149.1 0.1 broadcast_in_dim.53
  149.2 12.2 %all_to_all.28 = f32[4,16,16,256]{3,2,1,0:T(8,128)S(1)} all-to-all(f32[4,16,16,256]{3,2,1,0:T(8,128)S(1)} %broadcast_in_dim.53), channel_id=1, replica_groups=mesh['x'=4,'core'=2,'row'=4,'quad'=2,'place'=4] {'row'}, dimensions={0} | all-to-all | bytes 2097152 | tf_op jit(solution)/shard_map/all_to_all | solution.py:228
  161.4 0.1 copy.10
  161.5 11.3 %last_factor.1.own_ref = f32[384,256]{1,0:T(8,128)S(1)} custom-call(s32[1]{0:T(128)} %bitcast.17.col_ref, f32[1024,256]{1,0:T(8,128)S(1)} %bitcast.48, f32[1024,256]{1,0:T(8,128)S(1)} %next_factor.1.factor_ref), custom_call_target="tpu_custom_call" | custom-call | tf_op jit(solution)/shard_map/last_factor/pallas_call | solution.py:138
  172.8 11.6 %collective-permute-start.14 = (f32[384,256]{1,0:T(8,128)S(1)}, f32[384,256]{1,0:T(8,128)S(1)}, u32[]{:S(2)}, u32[]{:S(2)}) collective-permute-start(f32[384,256]{1,0:T(8,128)S(1)} %last_factor.1.own_ref), channel_id=1, source_target_pairs={{0,32},{32,0},{1,33},{33,1},{2,34},{34,2},{3,35},{35,3},{4,36},{36... | collective-permute-start | bytes 1179656 | tf_op jit(solution)/shard_map/ppermute | solution.py:290
  184.4 1.3 collective-permute-done.14.got_ref
  185.8 0.7 copy-done.6
  186.5 5.6 %outputs.1 = (f32[1,2,2048,128]{3,2,1,0:T(8,128)}, bf16[2,2048,128]{2,1,0:T(8,128)(2,1)}, f32[128,2,256]{2,1,0:T(2,128)}) custom-call(s32[1]{0:T(128)} %bitcast.core_ref, f32[4,2,512,256]{3,2,1,0:T(8,128)} %bitcast.49, f32[384,256]{1,0:T(8,128)} %copy-done.2, f32[384,256]{1,0:T(8,128)} %copy-done.6, f32[1,2,2048,128]{3,2,1,0:T(8,128)} %momentum_ref, ...), custom_call_target="tpu_custom_call" | custom-call | tf_op jit(solution)/shard_map/outputs/pallas_call | solution.py:185
  (26 shorter events, 0.3 us)
Async XLA Ops:
  7.2 1.0 copy-start
  7.2 8.9 %copy-start.3 = (f32[1,2,2048,128]{3,2,1,0:T(8,128)S(1)}, f32[1,2,2048,128]{3,2,1,0:T(8,128)}, u32[]{:S(2)}) copy-start(f32[1,2,2048,128]{3,2,1,0:T(8,128)} %momentum_ref) | copy-start | bytes 6291460
  7.2 62.9 %all-gather.4.cloned.1.call-start = ((), (), s32[]{:S(2)}) async-start(), calls=%async_computation.5 | async-start | bytes 1179648 | tf_op jit(solution)/shard_map/all_gather | solution.py:279
  10.4 5.7 %collective-permute-start = (f32[2048,128]{1,0:T(8,128)S(1)}, f32[2048,128]{1,0:T(8,128)}, u32[]{:S(2)}, u32[]{:S(2)}) collective-permute-start(f32[2048,128]{1,0:T(8,128)S(1)} %add_bitcast_fusion), channel_id=1, source_target_pairs={{0,32},{32,0},{1,33},{33,1},{2,34},{34,2},{3,35},{35,3},{4,36},{36... | collective-permute-start | bytes 3145736 | tf_op jit(solution)/shard_map/ppermute | solution.py:252
  17.7 9.5 %collective-permute-start.1 = (f32[512,128]{1,0:T(8,128)S(1)}, f32[512,128]{1,0:T(8,128)S(1)}, u32[]{:S(2)}, u32[]{:S(2)}) collective-permute-start(f32[512,128]{1,0:T(8,128)S(1)} %get-tuple-element.9), channel_id=1, source_target_pairs={{0,64},{64,128},{128,192},{192,0},{1,65},{65,129},{129,193},{193,1... | collective-permute-start | bytes 786440 | tf_op jit(solution)/shard_map/ppermute | solution.py:255
  17.8 13.6 %collective-permute-start.3 = (f32[512,128]{1,0:T(8,128)S(1)}, f32[512,128]{1,0:T(8,128)S(1)}, u32[]{:S(2)}, u32[]{:S(2)}) collective-permute-start(f32[512,128]{1,0:T(8,128)S(1)} %get-tuple-element.10), channel_id=1, source_target_pairs={{0,128},{64,192},{128,0},{192,64},{1,129},{65,193},{129,1},{193,65... | collective-permute-start | bytes 786440 | tf_op jit(solution)/shard_map/ppermute | solution.py:255
  19.7 12.7 %collective-permute-start.2 = (f32[512,128]{1,0:T(8,128)S(1)}, f32[512,128]{1,0:T(8,128)S(1)}, u32[]{:S(2)}, u32[]{:S(2)}) collective-permute-start(f32[512,128]{1,0:T(8,128)S(1)} %get-tuple-element.11), channel_id=1, source_target_pairs={{0,192},{64,0},{128,64},{192,128},{1,193},{65,1},{129,65},{193,129... | collective-permute-start | bytes 786440 | tf_op jit(solution)/shard_map/ppermute | solution.py:255
  32.4 12.8 %copy-start.4 = (f32[512,128]{1,0:T(8,128)}, f32[512,128]{1,0:T(8,128)S(1)}, u32[]{:S(2)}) copy-start(f32[512,128]{1,0:T(8,128)S(1)} %fusion.6) | copy-start | bytes 786436
  32.5 12.7 %collective-permute-start.4 = (f32[512,128]{1,0:T(8,128)S(1)}, f32[512,128]{1,0:T(8,128)S(1)}, u32[]{:S(2)}, u32[]{:S(2)}) collective-permute-start(f32[512,128]{1,0:T(8,128)S(1)} %fusion.6), channel_id=1, source_target_pairs={{0,1},{1,2},{2,3},{3,4},{4,5},{5,6},{6,7},{7,0},{8,9},{9,10},{10,1... | collective-permute-start | bytes 786440 | tf_op jit(solution)/shard_map/ppermute | solution.py:262
  33.1 12.1 %collective-permute-start.5 = (f32[512,128]{1,0:T(8,128)S(1)}, f32[512,128]{1,0:T(8,128)S(1)}, u32[]{:S(2)}, u32[]{:S(2)}) collective-permute-start(f32[512,128]{1,0:T(8,128)S(1)} %fusion.6), channel_id=1, source_target_pairs={{0,7},{1,0},{2,1},{3,2},{4,3},{5,4},{6,5},{7,6},{8,15},{9,8},{10,9... | collective-permute-start | bytes 786440 | tf_op jit(solution)/shard_map/ppermute | solution.py:265
  45.1 11.4 %collective-permute-start.6 = (f32[512,128]{1,0:T(8,128)S(1)}, f32[512,128]{1,0:T(8,128)S(1)}, u32[]{:S(2)}, u32[]{:S(2)}) collective-permute-start(f32[512,128]{1,0:T(8,128)S(1)} %collective-permute-done.4), channel_id=1, source_target_pairs={{0,1},{1,2},{2,3},{3,4},{4,5},{5,6},{6,7},{7,0},{8,9},{9,10},{10,1... | collective-permute-start | bytes 786440 | tf_op jit(solution)/shard_map/ppermute | solution.py:262
  45.2 11.4 %collective-permute-start.7 = (f32[512,128]{1,0:T(8,128)S(1)}, f32[512,128]{1,0:T(8,128)S(1)}, u32[]{:S(2)}, u32[]{:S(2)}) collective-permute-start(f32[512,128]{1,0:T(8,128)S(1)} %collective-permute-done.5), channel_id=1, source_target_pairs={{0,7},{1,0},{2,1},{3,2},{4,3},{5,4},{6,5},{7,6},{8,15},{9,8},{10,9... | collective-permute-start | bytes 786440 | tf_op jit(solution)/shard_map/ppermute | solution.py:265
  48.7 7.9 %copy-start.5 = (f32[512,128]{1,0:T(8,128)S(1)}, f32[512,128]{1,0:T(8,128)}, u32[]{:S(2)}) copy-start(f32[512,128]{1,0:T(8,128)} %copy-done.4) | copy-start | bytes 786436
  56.5 7.1 %collective-permute-start.8 = (f32[512,128]{1,0:T(8,128)S(1)}, f32[512,128]{1,0:T(8,128)S(1)}, u32[]{:S(2)}, u32[]{:S(2)}) collective-permute-start(f32[512,128]{1,0:T(8,128)S(1)} %collective-permute-done.6), channel_id=1, source_target_pairs={{0,1},{1,2},{2,3},{3,4},{4,5},{5,6},{6,7},{7,0},{8,9},{9,10},{10,1... | collective-permute-start | bytes 786440 | tf_op jit(solution)/shard_map/ppermute | solution.py:262
  56.6 7.1 %collective-permute-start.9 = (f32[512,128]{1,0:T(8,128)S(1)}, f32[512,128]{1,0:T(8,128)S(1)}, u32[]{:S(2)}, u32[]{:S(2)}) collective-permute-start(f32[512,128]{1,0:T(8,128)S(1)} %collective-permute-done.7), channel_id=1, source_target_pairs={{0,7},{1,0},{2,1},{3,2},{4,3},{5,4},{6,5},{7,6},{8,15},{9,8},{10,9... | collective-permute-start | bytes 786440 | tf_op jit(solution)/shard_map/ppermute | solution.py:265
  63.6 6.4 %collective-permute-start.10 = (f32[512,128]{1,0:T(8,128)S(1)}, f32[512,128]{1,0:T(8,128)S(1)}, u32[]{:S(2)}, u32[]{:S(2)}) collective-permute-start(f32[512,128]{1,0:T(8,128)S(1)} %collective-permute-done.8), channel_id=1, source_target_pairs={{0,1},{1,2},{2,3},{3,4},{4,5},{5,6},{6,7},{7,0},{8,9},{9,10},{10,1... | collective-permute-start | bytes 786440 | tf_op jit(solution)/shard_map/ppermute | solution.py:262
  74.8 15.5 %all-to-all-start = ((f32[16,16,256]{2,1,0:T(8,128)}), f32[16,16,256]{2,1,0:T(8,128)S(1)}, u32[]{:S(2)}, u32[]{:S(2)}) async-start(f32[16,16,256]{2,1,0:T(8,128)} %bitcast.9), calls=%async_computation | async-start | bytes 524288 | tf_op jit(solution)/shard_map/all_to_all | solution.py:236
  83.0 102.8 %all-gather.6.cloned.1.call-start = ((), (), s32[]{:S(2)}) async-start(), calls=%async_computation.6 | async-start | bytes 4718592 | tf_op jit(solution)/shard_map/all_gather | solution.py:287
  90.3 6.2 %collective-permute-start.13 = (f32[16,256]{1,0:T(8,128)S(1)}, f32[16,256]{1,0:T(8,128)S(1)}, u32[]{:S(2)}, u32[]{:S(2)}) collective-permute-start(f32[16,256]{1,0:T(8,128)S(1)} %reduce_sum.18), channel_id=1, source_target_pairs={{0,3},{1,0},{2,1},{3,2},{4,7},{5,4},{6,5},{7,6},{8,11},{9,8},{10,9... | collective-permute-start | bytes 49160 | tf_op jit(solution)/shard_map/ppermute | solution.py:221
  91.9 4.7 %collective-permute-start.12 = (f32[16,256]{1,0:T(8,128)S(1)}, f32[16,256]{1,0:T(8,128)S(1)}, u32[]{:S(2)}, u32[]{:S(2)}) collective-permute-start(f32[16,256]{1,0:T(8,128)S(1)} %reduce_sum.18), channel_id=1, source_target_pairs={{0,2},{1,3},{2,0},{3,1},{4,6},{5,7},{6,4},{7,5},{8,10},{9,11},{10,... | collective-permute-start | bytes 49160 | tf_op jit(solution)/shard_map/ppermute | solution.py:221
  92.2 4.4 %collective-permute-start.11 = (f32[16,256]{1,0:T(8,128)S(1)}, f32[16,256]{1,0:T(8,128)S(1)}, u32[]{:S(2)}, u32[]{:S(2)}) collective-permute-start(f32[16,256]{1,0:T(8,128)S(1)} %reduce_sum.18), channel_id=1, source_target_pairs={{0,1},{1,2},{2,3},{3,0},{4,5},{5,6},{6,7},{7,4},{8,9},{9,10},{10,1... | collective-permute-start | bytes 49160 | tf_op jit(solution)/shard_map/ppermute | solution.py:221
  96.7 15.5 %copy-start.1 = (f32[1024,256]{1,0:T(8,128)S(1)}, f32[1024,256]{1,0:T(8,128)}, u32[]{:S(2)}) copy-start(f32[1024,256]{1,0:T(8,128)} %all-gather.4.cloned.1.call-done.factor_ref) | copy-start | bytes 3145732
  172.8 13.0 %copy-start.2 = (f32[384,256]{1,0:T(8,128)}, f32[384,256]{1,0:T(8,128)S(1)}, u32[]{:S(2)}) copy-start(f32[384,256]{1,0:T(8,128)S(1)} %last_factor.1.own_ref) | copy-start | bytes 1179652
  172.8 13.0 %collective-permute-start.14 = (f32[384,256]{1,0:T(8,128)S(1)}, f32[384,256]{1,0:T(8,128)S(1)}, u32[]{:S(2)}, u32[]{:S(2)}) collective-permute-start(f32[384,256]{1,0:T(8,128)S(1)} %last_factor.1.own_ref), channel_id=1, source_target_pairs={{0,32},{32,0},{1,33},{33,1},{2,34},{34,2},{3,35},{35,3},{4,36},{36... | collective-permute-start | bytes 1179656 | tf_op jit(solution)/shard_map/ppermute | solution.py:290
  185.8 0.7 copy-start.6
Sparse Core Ops, SparseCore 0:
  21.0 38.2 all-gather.3
  125.9 40.2 all-gather.5

commit v3 on v2

--- a/solution.py
+++ b/solution.py
@@ -214,8 +214,8 @@
 
 def share_quad(share):
     place = lax.rem(lax.axis_index(COL), QUAD)
-    whole = jnp.zeros((QUAD,) + share.shape, share.dtype)
-    parts = [(0, share)]
+    whole = jnp.broadcast_to(share[None], (QUAD,) + share.shape)
+    parts = []
     for d in range(1, QUAD):
         pairs = [(k, k // QUAD * QUAD + (k + d) % QUAD) for k in range(NZ)]
         parts.append((QUAD - d, lax.ppermute(share, COL, pairs)))

time: 199 us -> 200 us (level)
  blocking collectives: 48.7 us -> 63.7 us
  waiting for transfers between devices: 52.5 us -> 44.9 us
  starting transfers between devices: 39.7 us -> 33.7 us
    all_to_all x1 -> x2, blocking collectives: 10.6 us -> 25.6 us  [sum_over_rows(): lax.all_to_all(partial.reshape(NX * NY, -1, RANK), ('x', 'row'), 0, 0)]
    all_to_all x1 -> x0, starting transfers between devices: 8.15 us -> none  [sum_over_rows(): lax.all_to_all(partial.reshape(NX * NY, -1, RANK), ('x', 'row'), 0, 0)]
    all_to_all x1 -> x0, waiting for transfers between devices: 7.23 us -> none  [sum_over_rows(): lax.all_to_all(partial.reshape(NX * NY, -1, RANK), ('x', 'row'), 0, 0)]
  transfers between devices with their start and end apart: 18 -> 17, of which waited for: 12 -> 12; matrix products, arithmetic and copies ran while one was open for 1% -> 1% of each run, Pallas kernels for 6% -> 6%
where the time goes in v3:
time: 200 us
  blocking collectives  63.7 us (32%)
  waiting for transfers between devices  44.9 us (22%)
  starting transfers between devices  33.7 us (17%)
  Pallas kernels  27.8 us (14%)
  between operations  14.4 us (7%)
  matrix products  8.7 us (4%)
  local copies, waits for them, and re-layouts  3.38 us (2%)
  other arithmetic  3.03 us (2%)
    all_to_all x3, blocking collectives, spread(): lax.all_to_all(jnp.broadcast_to(share[None], (size,) + share.shape), axes...  38.2 us
    ppermute x4, waiting for transfers between devices, gather_rows(): below = lax.ppermute(below, COL, up)  26.1 us
    all_to_all x2, blocking collectives, sum_over_rows(): lax.all_to_all(partial.reshape(NX * NY, -1, RANK), ('x', 'row'), 0, 0)  25.6 us
    ppermute x1, starting transfers between devices, shards(): got = lax.ppermute(sent, 'core', [(0, 1), (1, 0)])  12.9 us
    ppermute x3, waiting for transfers between devices, gather_rows(): came = [lax.ppermute(piece(d), 'x', ring(NX, d)) for d in (2, 1, 3)]  11.5 us
    pallas_call x1, Pallas kernels, last_factor(): pl.pallas_call(last_factor_kernel, in_specs=[pl.BlockSpec(memory_space=pl...  11.3 us
    pallas_call x1, Pallas kernels, next_factor(): pl.pallas_call(next_factor_kernel, out_shape=jax.ShapeDtypeStruct((KV, RA...  10.9 us
    ppermute x3, starting transfers between devices, gather_rows(): above = lax.ppermute(above, COL, down)  10.2 us
  transfers between devices with their start and end apart: 17, of which 12 were waited for; matrix products, arithmetic and copies ran while one was open for 1% of the time, Pallas kernels for 6%

profile of v3, /device:TPU:1, one launch (start us, length us, event | category | flops | bytes accessed | tf_op | source)
XLA Modules:
  0.0 199.6 jit_solution(6471571116905850181)
XLA Ops:
  7.2 0.0 copy-start
  7.2 0.0 copy-start.3
  7.2 0.0 all-gather.4.cloned.1.call-start
  7.2 0.9 copy-done
  8.1 0.1 constant_dynamic-slice_fusion
  8.2 0.7 copy.13
  8.9 1.4 add_bitcast_fusion
  10.4 3.3 %collective-permute-start = (f32[2048,128]{1,0:T(8,128)S(1)}, f32[2048,128]{1,0:T(8,128)}, u32[]{:S(2)}, u32[]{:S(2)}) collective-permute-start(f32[2048,128]{1,0:T(8,128)S(1)} %add_bitcast_fusion), channel_id=1, source_target_pairs={{0,32},{32,0},{1,33},{33,1},{2,34},{34,2},{3,35},{35,3},{4,36},{36... | collective-permute-start | bytes 3145736 | tf_op jit(solution)/shard_map/ppermute | solution.py:252
  13.7 2.4 %collective-permute-done = f32[2048,128]{1,0:T(8,128)} collective-permute-done((f32[2048,128]{1,0:T(8,128)S(1)}, f32[2048,128]{1,0:T(8,128)}, u32[]{:S(2)}, u32[]{:S(2)}) %collective-permute-start) | collective-permute-done | bytes 1048608 | tf_op jit(solution)/shard_map/ppermute | solution.py:252
  16.1 1.5 bitcast_add_fusion
  17.6 0.1 dynamic-slice_bitcast_fusion.2
  17.7 0.1 collective-permute-start.1
  17.8 1.9 collective-permute-start.3
  19.7 1.2 collective-permute-start.2
  20.8 0.0 all-gather.4.cloned.1.call-update
  20.8 0.0 all-gather.6.cloned.1.call-start
  20.9 6.3 %collective-permute-done.1 = f32[512,128]{1,0:T(8,128)S(1)} collective-permute-done((f32[512,128]{1,0:T(8,128)S(1)}, f32[512,128]{1,0:T(8,128)S(1)}, u32[]{:S(2)}, u32[]{:S(2)}) %collective-permute-start.1) | collective-permute-done | bytes 262176 | tf_op jit(solution)/shard_map/ppermute | solution.py:255
  27.2 4.2 %collective-permute-done.3 = f32[512,128]{1,0:T(8,128)S(1)} collective-permute-done((f32[512,128]{1,0:T(8,128)S(1)}, f32[512,128]{1,0:T(8,128)S(1)}, u32[]{:S(2)}, u32[]{:S(2)}) %collective-permute-start.3) | collective-permute-done | bytes 262176 | tf_op jit(solution)/shard_map/ppermute | solution.py:255
  31.4 1.0 collective-permute-done.2
  32.4 0.1 fusion.6
  32.4 0.0 copy-start.4
  32.5 0.7 collective-permute-start.4
  33.1 4.0 %collective-permute-start.5 = (f32[512,128]{1,0:T(8,128)S(1)}, f32[512,128]{1,0:T(8,128)S(1)}, u32[]{:S(2)}, u32[]{:S(2)}) collective-permute-start(f32[512,128]{1,0:T(8,128)S(1)} %fusion.6), channel_id=1, source_target_pairs={{0,7},{1,0},{2,1},{3,2},{4,3},{5,4},{6,5},{7,6},{8,15},{9,8},{10,9... | collective-permute-start | bytes 786440 | tf_op jit(solution)/shard_map/ppermute | solution.py:265
  37.1 8.0 %collective-permute-done.4 = f32[512,128]{1,0:T(8,128)S(1)} collective-permute-done((f32[512,128]{1,0:T(8,128)S(1)}, f32[512,128]{1,0:T(8,128)S(1)}, u32[]{:S(2)}, u32[]{:S(2)}) %collective-permute-start.4) | collective-permute-done | bytes 262176 | tf_op jit(solution)/shard_map/ppermute | solution.py:262
  45.1 0.0 collective-permute-start.6
  45.1 0.1 collective-permute-done.5
  45.2 3.5 %collective-permute-start.7 = (f32[512,128]{1,0:T(8,128)S(1)}, f32[512,128]{1,0:T(8,128)S(1)}, u32[]{:S(2)}, u32[]{:S(2)}) collective-permute-start(f32[512,128]{1,0:T(8,128)S(1)} %collective-permute-done.5), channel_id=1, source_target_pairs={{0,7},{1,0},{2,1},{3,2},{4,3},{5,4},{6,5},{7,6},{8,15},{9,8},{10,9... | collective-permute-start | bytes 786440 | tf_op jit(solution)/shard_map/ppermute | solution.py:265
  48.7 0.2 broadcast_in_dim.44
  49.0 7.5 %collective-permute-done.6 = f32[512,128]{1,0:T(8,128)S(1)} collective-permute-done((f32[512,128]{1,0:T(8,128)S(1)}, f32[512,128]{1,0:T(8,128)S(1)}, u32[]{:S(2)}, u32[]{:S(2)}) %collective-permute-start.6) | collective-permute-done | bytes 262176 | tf_op jit(solution)/shard_map/ppermute | solution.py:262
  56.5 0.0 collective-permute-start.8
  56.5 0.0 copy-done.5
  56.6 0.0 collective-permute-done.7
  56.6 2.7 %collective-permute-start.9 = (f32[512,128]{1,0:T(8,128)S(1)}, f32[512,128]{1,0:T(8,128)S(1)}, u32[]{:S(2)}, u32[]{:S(2)}) collective-permute-start(f32[512,128]{1,0:T(8,128)S(1)} %collective-permute-done.7), channel_id=1, source_target_pairs={{0,7},{1,0},{2,1},{3,2},{4,3},{5,4},{6,5},{7,6},{8,15},{9,8},{10,9... | collective-permute-start | bytes 786440 | tf_op jit(solution)/shard_map/ppermute | solution.py:265
  59.4 4.2 %collective-permute-done.8 = f32[512,128]{1,0:T(8,128)S(1)} collective-permute-done((f32[512,128]{1,0:T(8,128)S(1)}, f32[512,128]{1,0:T(8,128)S(1)}, u32[]{:S(2)}, u32[]{:S(2)}) %collective-permute-start.8) | collective-permute-done | bytes 262176 | tf_op jit(solution)/shard_map/ppermute | solution.py:262
  63.6 0.0 collective-permute-start.10
  63.7 0.0 collective-permute-done.9
  63.7 6.3 %collective-permute-done.10 = f32[512,128]{1,0:T(8,128)S(1)} collective-permute-done((f32[512,128]{1,0:T(8,128)S(1)}, f32[512,128]{1,0:T(8,128)S(1)}, u32[]{:S(2)}, u32[]{:S(2)}) %collective-permute-start.10) | collective-permute-done | bytes 262176 | tf_op jit(solution)/shard_map/ppermute | solution.py:262
  70.0 0.0 all-gather.4.cloned.1.call-done.factor_ref
  70.1 3.0 %fusion.9 = f32[512,256]{1,0:T(8,128)S(1)} fusion(f32[512,1024]{1,0:T(8,128)S(1)} %constant_dynamic-update-slice_fusion, f32[1024,256]{1,0:T(8,128)} %all-gather.4.cloned.1.call-done.factor_ref), kind=kOutput, calls=%fused_computation.28 | convolution fusion | flops 1610612736 | bytes 3670016 | tf_op jit(solution)/shard_map/dot_general | solution.py:27
  73.1 1.0 fusion.2
  74.1 15.3 %all_to_all.25 = f32[16,16,256]{2,1,0:T(8,128)S(1)} all-to-all(f32[16,16,256]{2,1,0:T(8,128)S(1)} %bitcast.53), channel_id=1, replica_groups=mesh['x'=4,'core'=2,'row'=4,'quad'=2,'place'=4] {'x','row'}, dimensions={0} | all-to-all | bytes 524288 | tf_op jit(solution)/shard_map/all_to_all | solution.py:236
  89.4 0.7 collective-permute-start.11
  90.1 2.7 %collective-permute-start.13 = (f32[16,256]{1,0:T(8,128)S(1)}, f32[16,256]{1,0:T(8,128)S(1)}, u32[]{:S(2)}, u32[]{:S(2)}) collective-permute-start(f32[16,256]{1,0:T(8,128)S(1)} %reduce_sum.18), channel_id=1, source_target_pairs={{0,3},{1,0},{2,1},{3,2},{4,7},{5,4},{6,5},{7,6},{8,11},{9,8},{10,9... | collective-permute-start | bytes 49160 | tf_op jit(solution)/shard_map/ppermute | solution.py:221
  92.8 0.0 collective-permute-start.12
  92.8 1.4 collective-permute-done.11
  94.2 2.1 %collective-permute-done.12 = f32[16,256]{1,0:T(8,128)S(1)} collective-permute-done((f32[16,256]{1,0:T(8,128)S(1)}, f32[16,256]{1,0:T(8,128)S(1)}, u32[]{:S(2)}, u32[]{:S(2)}) %collective-permute-start.12) | collective-permute-done | bytes 16416 | tf_op jit(solution)/shard_map/ppermute | solution.py:221
  96.3 0.0 collective-permute-done.13
  96.3 0.1 broadcast_in_dim.49
  96.4 15.1 %all_to_all.26 = f32[16,4,16,256]{3,2,1,0:T(8,128)S(1)} all-to-all(f32[16,4,16,256]{3,2,1,0:T(8,128)S(1)} %broadcast_in_dim.49), channel_id=1, replica_groups=mesh['x'=4,'core'=2,'row'=4,'quad'=2,'place'=4] {'x','row'}, dimensions={0} | all-to-all | bytes 2097152 | tf_op jit(solution)/shard_map/all_to_all | solution.py:228
  111.5 0.1 copy.9
  111.6 10.9 %next_factor.1.factor_ref = f32[1024,256]{1,0:T(8,128)S(1)} custom-call(f32[1024,256]{1,0:T(8,128)S(1)} %bitcast.45, f32[1024,256]{1,0:T(8,128)S(1)} %copy-done.1), custom_call_target="tpu_custom_call" | custom-call | tf_op jit(solution)/shard_map/next_factor/pallas_call | solution.py:127
  122.5 2.6 %fusion.10 = f32[512,256]{1,0:T(8,128)} fusion(f32[512,1024]{1,0:T(8,128)S(1)} %constant_dynamic-update-slice_fusion, f32[1024,256]{1,0:T(8,128)S(1)} %next_factor.1.factor_ref), kind=kOutput, calls=%fused_computation.29 | convolution fusion | flops 1610612736 | bytes 3670016 | tf_op jit(solution)/shard_map/dot_general | solution.py:27
  125.1 0.0 all-gather.6.cloned.1.call-update
  125.2 2.1 %fusion = f32[256,256]{1,0:T(8,128)S(1)} fusion(f32[512,256]{1,0:T(8,128)} %fusion.10, f32[512,1024]{1,0:T(8,128)S(1)} %constant_dynamic-update-slice_fusion, s32[]{:T(128)S(6)} %select_n.77), kind=kOutput, calls=%fused_computation.2 | convolution fusion | flops 402653184 | bytes 1310724 | tf_op jit(solution)/shard_map/dot_general | solution.py:27
  127.2 10.3 %all_to_all.27 = f32[16,16,256]{2,1,0:T(8,128)S(1)} all-to-all(f32[16,16,256]{2,1,0:T(8,128)S(1)} %bitcast.52), channel_id=1, replica_groups=mesh['x'=4,'core'=2,'row'=4,'quad'=2,'place'=4] {'x','row'}, dimensions={0} | all-to-all | bytes 524288 | tf_op jit(solution)/shard_map/all_to_all | solution.py:236
  137.5 10.9 %all_to_all.28 = f32[16,16,256]{2,1,0:T(8,128)S(1)} all-to-all(f32[16,16,256]{2,1,0:T(8,128)S(1)} %broadcast_in_dim.51), channel_id=1, replica_groups=mesh['x'=4,'core'=2,'row'=4,'quad'=2,'place'=4] {'x','place'}, dimensions={0} | all-to-all | bytes 524288 | tf_op jit(solution)/shard_map/all_to_all | solution.py:228
  148.4 0.1 broadcast_in_dim.52
  148.6 12.2 %all_to_all.29 = f32[4,16,16,256]{3,2,1,0:T(8,128)S(1)} all-to-all(f32[4,16,16,256]{3,2,1,0:T(8,128)S(1)} %broadcast_in_dim.52), channel_id=1, replica_groups=mesh['x'=4,'core'=2,'row'=4,'quad'=2,'place'=4] {'row'}, dimensions={0} | all-to-all | bytes 2097152 | tf_op jit(solution)/shard_map/all_to_all | solution.py:228
  160.8 0.1 copy.10
  160.9 11.3 %last_factor.1.own_ref = f32[384,256]{1,0:T(8,128)S(1)} custom-call(s32[1]{0:T(128)} %bitcast.16.col_ref, f32[1024,256]{1,0:T(8,128)S(1)} %bitcast.46, f32[1024,256]{1,0:T(8,128)S(1)} %next_factor.1.factor_ref), custom_call_target="tpu_custom_call" | custom-call | tf_op jit(solution)/shard_map/last_factor/pallas_call | solution.py:138
  172.2 12.9 %collective-permute-start.14 = (f32[384,256]{1,0:T(8,128)S(1)}, f32[384,256]{1,0:T(8,128)S(1)}, u32[]{:S(2)}, u32[]{:S(2)}) collective-permute-start(f32[384,256]{1,0:T(8,128)S(1)} %last_factor.1.own_ref), channel_id=1, source_target_pairs={{0,32},{32,0},{1,33},{33,1},{2,34},{34,2},{3,35},{35,3},{4,36},{36... | collective-permute-start | bytes 1179656 | tf_op jit(solution)/shard_map/ppermute | solution.py:290
  185.1 1.3 collective-permute-done.14.got_ref
  186.4 0.7 copy-done.6
  187.2 5.6 %outputs.1 = (f32[1,2,2048,128]{3,2,1,0:T(8,128)}, bf16[2,2048,128]{2,1,0:T(8,128)(2,1)}, f32[128,2,256]{2,1,0:T(2,128)}) custom-call(s32[1]{0:T(128)} %bitcast.core_ref, f32[4,2,512,256]{3,2,1,0:T(8,128)} %bitcast.47, f32[384,256]{1,0:T(8,128)} %copy-done.2, f32[384,256]{1,0:T(8,128)} %copy-done.6, f32[1,2,2048,128]{3,2,1,0:T(8,128)} %momentum_ref, ...), custom_call_target="tpu_custom_call" | custom-call | tf_op jit(solution)/shard_map/outputs/pallas_call | solution.py:185
  (24 shorter events, 0.3 us)
Async XLA Ops:
  7.2 1.0 copy-start
  7.2 8.9 %copy-start.3 = (f32[1,2,2048,128]{3,2,1,0:T(8,128)S(1)}, f32[1,2,2048,128]{3,2,1,0:T(8,128)}, u32[]{:S(2)}) copy-start(f32[1,2,2048,128]{3,2,1,0:T(8,128)} %momentum_ref) | copy-start | bytes 6291460
  7.2 62.9 %all-gather.4.cloned.1.call-start = ((), (), s32[]{:S(2)}) async-start(), calls=%async_computation.5 | async-start | bytes 1179648 | tf_op jit(solution)/shard_map/all_gather | solution.py:279
  10.4 5.7 %collective-permute-start = (f32[2048,128]{1,0:T(8,128)S(1)}, f32[2048,128]{1,0:T(8,128)}, u32[]{:S(2)}, u32[]{:S(2)}) collective-permute-start(f32[2048,128]{1,0:T(8,128)S(1)} %add_bitcast_fusion), channel_id=1, source_target_pairs={{0,32},{32,0},{1,33},{33,1},{2,34},{34,2},{3,35},{35,3},{4,36},{36... | collective-permute-start | bytes 3145736 | tf_op jit(solution)/shard_map/ppermute | solution.py:252
  17.7 9.5 %collective-permute-start.1 = (f32[512,128]{1,0:T(8,128)S(1)}, f32[512,128]{1,0:T(8,128)S(1)}, u32[]{:S(2)}, u32[]{:S(2)}) collective-permute-start(f32[512,128]{1,0:T(8,128)S(1)} %get-tuple-element.9), channel_id=1, source_target_pairs={{0,64},{64,128},{128,192},{192,0},{1,65},{65,129},{129,193},{193,1... | collective-permute-start | bytes 786440 | tf_op jit(solution)/shard_map/ppermute | solution.py:255
  17.8 13.6 %collective-permute-start.3 = (f32[512,128]{1,0:T(8,128)S(1)}, f32[512,128]{1,0:T(8,128)S(1)}, u32[]{:S(2)}, u32[]{:S(2)}) collective-permute-start(f32[512,128]{1,0:T(8,128)S(1)} %get-tuple-element.10), channel_id=1, source_target_pairs={{0,128},{64,192},{128,0},{192,64},{1,129},{65,193},{129,1},{193,65... | collective-permute-start | bytes 786440 | tf_op jit(solution)/shard_map/ppermute | solution.py:255
  19.7 12.7 %collective-permute-start.2 = (f32[512,128]{1,0:T(8,128)S(1)}, f32[512,128]{1,0:T(8,128)S(1)}, u32[]{:S(2)}, u32[]{:S(2)}) collective-permute-start(f32[512,128]{1,0:T(8,128)S(1)} %get-tuple-element.11), channel_id=1, source_target_pairs={{0,192},{64,0},{128,64},{192,128},{1,193},{65,1},{129,65},{193,129... | collective-permute-start | bytes 786440 | tf_op jit(solution)/shard_map/ppermute | solution.py:255
  20.8 165.6 %all-gather.6.cloned.1.call-start = ((), (), s32[]{:S(2)}) async-start(), calls=%async_computation.6 | async-start | bytes 4718592 | tf_op jit(solution)/shard_map/all_gather | solution.py:287
  32.4 12.8 %copy-start.4 = (f32[512,128]{1,0:T(8,128)}, f32[512,128]{1,0:T(8,128)S(1)}, u32[]{:S(2)}) copy-start(f32[512,128]{1,0:T(8,128)S(1)} %fusion.6) | copy-start | bytes 786436
  32.5 12.7 %collective-permute-start.4 = (f32[512,128]{1,0:T(8,128)S(1)}, f32[512,128]{1,0:T(8,128)S(1)}, u32[]{:S(2)}, u32[]{:S(2)}) collective-permute-start(f32[512,128]{1,0:T(8,128)S(1)} %fusion.6), channel_id=1, source_target_pairs={{0,1},{1,2},{2,3},{3,4},{4,5},{5,6},{6,7},{7,0},{8,9},{9,10},{10,1... | collective-permute-start | bytes 786440 | tf_op jit(solution)/shard_map/ppermute | solution.py:262
  33.1 12.1 %collective-permute-start.5 = (f32[512,128]{1,0:T(8,128)S(1)}, f32[512,128]{1,0:T(8,128)S(1)}, u32[]{:S(2)}, u32[]{:S(2)}) collective-permute-start(f32[512,128]{1,0:T(8,128)S(1)} %fusion.6), channel_id=1, source_target_pairs={{0,7},{1,0},{2,1},{3,2},{4,3},{5,4},{6,5},{7,6},{8,15},{9,8},{10,9... | collective-permute-start | bytes 786440 | tf_op jit(solution)/shard_map/ppermute | solution.py:265
  45.1 11.4 %collective-permute-start.6 = (f32[512,128]{1,0:T(8,128)S(1)}, f32[512,128]{1,0:T(8,128)S(1)}, u32[]{:S(2)}, u32[]{:S(2)}) collective-permute-start(f32[512,128]{1,0:T(8,128)S(1)} %collective-permute-done.4), channel_id=1, source_target_pairs={{0,1},{1,2},{2,3},{3,4},{4,5},{5,6},{6,7},{7,0},{8,9},{9,10},{10,1... | collective-permute-start | bytes 786440 | tf_op jit(solution)/shard_map/ppermute | solution.py:262
  45.2 11.4 %collective-permute-start.7 = (f32[512,128]{1,0:T(8,128)S(1)}, f32[512,128]{1,0:T(8,128)S(1)}, u32[]{:S(2)}, u32[]{:S(2)}) collective-permute-start(f32[512,128]{1,0:T(8,128)S(1)} %collective-permute-done.5), channel_id=1, source_target_pairs={{0,7},{1,0},{2,1},{3,2},{4,3},{5,4},{6,5},{7,6},{8,15},{9,8},{10,9... | collective-permute-start | bytes 786440 | tf_op jit(solution)/shard_map/ppermute | solution.py:265
  48.7 7.9 %copy-start.5 = (f32[512,128]{1,0:T(8,128)S(1)}, f32[512,128]{1,0:T(8,128)}, u32[]{:S(2)}) copy-start(f32[512,128]{1,0:T(8,128)} %copy-done.4) | copy-start | bytes 786436
  56.5 7.1 %collective-permute-start.8 = (f32[512,128]{1,0:T(8,128)S(1)}, f32[512,128]{1,0:T(8,128)S(1)}, u32[]{:S(2)}, u32[]{:S(2)}) collective-permute-start(f32[512,128]{1,0:T(8,128)S(1)} %collective-permute-done.6), channel_id=1, source_target_pairs={{0,1},{1,2},{2,3},{3,4},{4,5},{5,6},{6,7},{7,0},{8,9},{9,10},{10,1... | collective-permute-start | bytes 786440 | tf_op jit(solution)/shard_map/ppermute | solution.py:262
  56.6 7.1 %collective-permute-start.9 = (f32[512,128]{1,0:T(8,128)S(1)}, f32[512,128]{1,0:T(8,128)S(1)}, u32[]{:S(2)}, u32[]{:S(2)}) collective-permute-start(f32[512,128]{1,0:T(8,128)S(1)} %collective-permute-done.7), channel_id=1, source_target_pairs={{0,7},{1,0},{2,1},{3,2},{4,3},{5,4},{6,5},{7,6},{8,15},{9,8},{10,9... | collective-permute-start | bytes 786440 | tf_op jit(solution)/shard_map/ppermute | solution.py:265
  63.6 6.4 %collective-permute-start.10 = (f32[512,128]{1,0:T(8,128)S(1)}, f32[512,128]{1,0:T(8,128)S(1)}, u32[]{:S(2)}, u32[]{:S(2)}) collective-permute-start(f32[512,128]{1,0:T(8,128)S(1)} %collective-permute-done.8), channel_id=1, source_target_pairs={{0,1},{1,2},{2,3},{3,4},{4,5},{5,6},{6,7},{7,0},{8,9},{9,10},{10,1... | collective-permute-start | bytes 786440 | tf_op jit(solution)/shard_map/ppermute | solution.py:262
  89.4 4.8 %collective-permute-start.11 = (f32[16,256]{1,0:T(8,128)S(1)}, f32[16,256]{1,0:T(8,128)S(1)}, u32[]{:S(2)}, u32[]{:S(2)}) collective-permute-start(f32[16,256]{1,0:T(8,128)S(1)} %reduce_sum.18), channel_id=1, source_target_pairs={{0,1},{1,2},{2,3},{3,0},{4,5},{5,6},{6,7},{7,4},{8,9},{9,10},{10,1... | collective-permute-start | bytes 49160 | tf_op jit(solution)/shard_map/ppermute | solution.py:221
  90.1 6.2 %collective-permute-start.13 = (f32[16,256]{1,0:T(8,128)S(1)}, f32[16,256]{1,0:T(8,128)S(1)}, u32[]{:S(2)}, u32[]{:S(2)}) collective-permute-start(f32[16,256]{1,0:T(8,128)S(1)} %reduce_sum.18), channel_id=1, source_target_pairs={{0,3},{1,0},{2,1},{3,2},{4,7},{5,4},{6,5},{7,6},{8,11},{9,8},{10,9... | collective-permute-start | bytes 49160 | tf_op jit(solution)/shard_map/ppermute | solution.py:221
  92.8 3.5 %collective-permute-start.12 = (f32[16,256]{1,0:T(8,128)S(1)}, f32[16,256]{1,0:T(8,128)S(1)}, u32[]{:S(2)}, u32[]{:S(2)}) collective-permute-start(f32[16,256]{1,0:T(8,128)S(1)} %reduce_sum.18), channel_id=1, source_target_pairs={{0,2},{1,3},{2,0},{3,1},{4,6},{5,7},{6,4},{7,5},{8,10},{9,11},{10,... | collective-permute-start | bytes 49160 | tf_op jit(solution)/shard_map/ppermute | solution.py:221
  96.4 15.2 %copy-start.1 = (f32[1024,256]{1,0:T(8,128)S(1)}, f32[1024,256]{1,0:T(8,128)}, u32[]{:S(2)}) copy-start(f32[1024,256]{1,0:T(8,128)} %all-gather.4.cloned.1.call-done.factor_ref) | copy-start | bytes 3145732
  172.2 14.3 %copy-start.2 = (f32[384,256]{1,0:T(8,128)}, f32[384,256]{1,0:T(8,128)S(1)}, u32[]{:S(2)}) copy-start(f32[384,256]{1,0:T(8,128)S(1)} %last_factor.1.own_ref) | copy-start | bytes 1179652
  172.2 14.2 %collective-permute-start.14 = (f32[384,256]{1,0:T(8,128)S(1)}, f32[384,256]{1,0:T(8,128)S(1)}, u32[]{:S(2)}, u32[]{:S(2)}) collective-permute-start(f32[384,256]{1,0:T(8,128)S(1)} %last_factor.1.own_ref), channel_id=1, source_target_pairs={{0,32},{32,0},{1,33},{33,1},{2,34},{34,2},{3,35},{35,3},{4,36},{36... | collective-permute-start | bytes 1179656 | tf_op jit(solution)/shard_map/ppermute | solution.py:290
  186.4 0.7 copy-start.6
Sparse Core Ops, SparseCore 0:
  21.0 38.2 all-gather.3
  125.3 41.4 all-gather.5
